TPU v7x, 32 devices: a whole 2x2x4 slice. The times are simulated.
32 devices in a mesh: band: 16 (over z, x, core), grp: 2 (over y).
Axes of the slice: x: 2, y: 2, z: 4, core: 2. Of those that a mesh axis runs over, the one named last changes fastest.
Arguments:
- tokens: bfloat16 [4, 2048, 1024], P('grp', 'band'), may hold values from -6 to 6
- lead_index: int32 [4, 2], P('grp'), may hold values from 1 to 40
- segment: int32 [4, 2048], P('grp'), may hold values from 0 to 1, as said below
- valid: int32 [4, 2048], P('grp'), may hold values from 0 to 1, as said below
- lead_weight: float32 [1024], replicated, may hold values from -4 to 4
- lead_bias: float32 [1024], replicated, may hold values from -6 to 6
- first_gain: float32 [1024], replicated, may hold values from 0.5 to 1.5
- first_shift: float32 [1024], replicated, may hold values from -6 to 6
- heads_weight: bfloat16 [1024, 3072], replicated, may hold values from -0.25 to 0.25
- query_bias: float32 [1024], replicated, may hold values from -6 to 6
- value_bias: float32 [1024], replicated, may hold values from -6 to 6
- output_weight: bfloat16 [1024, 1024], replicated, may hold values from -1.5 to 1.5
- output_bias: float32 [1024], replicated, may hold values from -6 to 6
- second_gain: float32 [1024], replicated, may hold values from 0.5 to 1.5
- second_shift: float32 [1024], replicated, may hold values from -6 to 6
- up_weight: bfloat16 [1024, 4096], replicated, may hold values from -0.1875 to 0.1875
- up_bias: float32 [4096], replicated, may hold values from -6 to 6
- down_weight: bfloat16 [4096, 1024], replicated, may hold values from -0.125 to 0.125
- down_bias: float32 [1024], replicated, may hold values from -6 to 6
- cotangent: bfloat16 [4, 2048, 1024], P('grp', 'band'), may hold values from -6 to 6
Outputs:
- result: bfloat16 [4, 2048, 1024], P('grp', 'band')
- grad_tokens: float32 [4, 2048, 1024], P('grp', 'band')
- grad_lead_weight: float32 [1024], P('band')
- grad_lead_bias: float32 [1024], P('band')
- grad_first_gain: float32 [1024], P('band')
- grad_first_shift: float32 [1024], P('band')
- grad_heads_weight: float32 [1024, 3072], P('band')
- grad_query_bias: float32 [1024], P('band')
- grad_value_bias: float32 [1024], P('band')
- grad_output_weight: float32 [1024, 1024], P('band')
- grad_output_bias: float32 [1024], P('band')
- grad_second_gain: float32 [1024], P('band')
- grad_second_shift: float32 [1024], P('band')
- grad_up_weight: float32 [1024, 4096], P('band')
- grad_up_bias: float32 [4096], P('band')
- grad_down_weight: float32 [4096, 1024], P('band')
- grad_down_bias: float32 [1024], P('band')
Inputs may be any that keep to these rules, and one draw needn't show every extreme that they name: `segment`: A group holds one sample (all rows 0) or two; in a two-sample group, within each aligned run of 128 rows the first half is sample 0 and the second half sample 1. Half of the groups hold two samples. Padding lies at the end of a sample's rows within each aligned run of 128 rows, at most 16 rows there; the first row of a sample in each run is valid. `lead_index`: the second entry of a group is read only where the group holds two samples.
All inputs are finite; a program needn't handle non-finite values.
Results may differ from a plain program's by a relative error of at most 0.02.
Values may be sent and summed in bfloat16 or wider, within the bound.
A program may use at most 320 MiB of HBM per device.

v0:
```python
import jax
import jax.numpy as jnp
from jax import lax
from jax.sharding import PartitionSpec as P

HEADS = 16
HEAD_DIM = 64


def layer_norm(values, gain, shift):
    center = values - jnp.mean(values, -1, keepdims=True)
    spread = jnp.mean(center * center, -1, keepdims=True)
    return center * lax.rsqrt(spread + 1e-05) * gain + shift


def gelu_exact(values):
    return jax.nn.gelu(values, approximate=False)


def head_split(array):
    return array.reshape(array.shape[0], HEADS, HEAD_DIM)


def masked_scores(query_rows, key_rows, query_seg, key_seg, key_valid):
    scores = jnp.einsum(
        "rhd,khd->hrk",
        head_split(query_rows),
        head_split(key_rows),
        preferred_element_type=jnp.float32,
    ) * HEAD_DIM ** (-0.5)
    allowed = (query_seg[:, None] == key_seg[None, :]) & (key_valid[None, :] == 1)
    return (scores, allowed[None])


def local(
    tokens,
    lead_index,
    segment,
    valid,
    lead_weight,
    lead_bias,
    first_gain,
    first_shift,
    heads_weight,
    query_bias,
    value_bias,
    output_weight,
    output_bias,
    second_gain,
    second_shift,
    up_weight,
    up_bias,
    down_weight,
    down_bias,
    cotangent,
):
    groups, rows, width = tokens.shape
    group_rows = segment.shape[1]
    total = groups * rows
    scale = HEAD_DIM ** (-0.5)
    band_start = lax.axis_index("band") * rows
    local_seg = lax.dynamic_slice_in_dim(segment, band_start, rows, 1)
    lead_days = lead_index.astype(jnp.float32) * 0.25
    lead_rows = jnp.where(local_seg == 0, lead_days[:, 0:1], lead_days[:, 1:2]).reshape(total, 1)
    start = tokens.reshape(total, width).astype(jnp.float32) + lead_rows * lead_weight + lead_bias
    first_norm, first_back = jax.vjp(layer_norm, start, first_gain, first_shift)
    first_low = first_norm.astype(jnp.bfloat16)
    joined = jnp.dot(first_low, heads_weight, preferred_element_type=jnp.float32) + jnp.concatenate(
        [query_bias, jnp.zeros_like(query_bias), value_bias]
    )
    query_flat = joined[:, :width].astype(jnp.bfloat16)
    key_flat = joined[:, width : 2 * width].astype(jnp.bfloat16)
    value_flat = joined[:, 2 * width :].astype(jnp.bfloat16)
    query = query_flat.reshape(groups, rows, width)
    local_keys = key_flat.reshape(groups, rows, width)
    local_values = value_flat.reshape(groups, rows, width)
    key_all, value_all = (
        lax.all_gather(local_keys, "band", axis=1, tiled=True),
        lax.all_gather(local_values, "band", axis=1, tiled=True),
    )

    def attend(items):
        query_rows, key_rows, value_rows, query_seg, key_seg, key_valid = items
        scores, allowed = masked_scores(query_rows, key_rows, query_seg, key_seg, key_valid)
        scores = jnp.where(allowed, scores, -1e30)
        peak = jnp.max(scores, -1, keepdims=True)
        shifted = jnp.exp(scores - peak)
        totals = jnp.sum(shifted, -1, keepdims=True)
        probs = (shifted / totals).astype(jnp.bfloat16)
        mixed = jnp.einsum(
            "hrk,khd->rhd", probs, head_split(value_rows), preferred_element_type=jnp.float32
        )
        return (mixed.reshape(rows, width).astype(jnp.bfloat16), peak + jnp.log(totals))

    attended, logsum = lax.map(attend, (query, key_all, value_all, local_seg, segment, valid))
    attended = attended.reshape(total, width)
    middle = (
        start + jnp.dot(attended, output_weight, preferred_element_type=jnp.float32) + output_bias
    )
    second_norm, second_back = jax.vjp(layer_norm, middle, second_gain, second_shift)
    second_low = second_norm.astype(jnp.bfloat16)
    upper = jnp.dot(second_low, up_weight, preferred_element_type=jnp.float32) + up_bias
    active, gelu_back = jax.vjp(gelu_exact, upper)
    hidden = active.astype(jnp.bfloat16)
    outcome = (
        (middle + jnp.dot(hidden, down_weight, preferred_element_type=jnp.float32) + down_bias)
        .astype(jnp.bfloat16)
        .reshape(groups, rows, width)
    )
    grad_out = cotangent.reshape(total, width)
    grad_down = jnp.einsum("tf,td->fd", hidden, grad_out, preferred_element_type=jnp.float32)
    grad_down_bias = jnp.sum(grad_out.astype(jnp.float32), 0)
    grad_hidden = jnp.einsum("td,fd->tf", grad_out, down_weight, preferred_element_type=jnp.float32)
    grad_upper = gelu_back(grad_hidden)[0].astype(jnp.bfloat16)
    grad_up = jnp.einsum("td,tf->df", second_low, grad_upper, preferred_element_type=jnp.float32)
    grad_up_bias = jnp.sum(grad_upper.astype(jnp.float32), 0)
    grad_second = jnp.einsum("tf,df->td", grad_upper, up_weight, preferred_element_type=jnp.float32)
    grad_middle, grad_second_gain, grad_second_shift = second_back(grad_second)
    grad_middle = grad_middle + grad_out.astype(jnp.float32)
    grad_branch = grad_middle.astype(jnp.bfloat16)
    grad_output = jnp.einsum("td,te->de", attended, grad_branch, preferred_element_type=jnp.float32)
    grad_output_bias = jnp.sum(grad_branch.astype(jnp.float32), 0)
    grad_attended = jnp.einsum(
        "te,de->td", grad_branch, output_weight, preferred_element_type=jnp.float32
    ).astype(jnp.bfloat16)
    key_back, value_back = (key_all, value_all)

    def attend_back(carry, items):
        query_rows, key_rows, value_rows, query_seg, key_seg, key_valid, logsum_rows, grad_rows = (
            items
        )
        scores, allowed = masked_scores(query_rows, key_rows, query_seg, key_seg, key_valid)
        probs = jnp.where(allowed, jnp.exp(scores - logsum_rows), 0.0)
        grad_heads = head_split(grad_rows)
        grad_probs = jnp.einsum(
            "rhd,khd->hrk", grad_heads, head_split(value_rows), preferred_element_type=jnp.float32
        )
        grad_scores = (
            probs * (grad_probs - jnp.sum(probs * grad_probs, -1, keepdims=True))
        ).astype(jnp.bfloat16)
        grad_query_rows = (
            jnp.einsum(
                "hrk,khd->rhd",
                grad_scores,
                head_split(key_rows),
                preferred_element_type=jnp.float32,
            )
            * scale
        )
        key_term = (
            jnp.einsum(
                "hrk,rhd->khd",
                grad_scores,
                head_split(query_rows),
                preferred_element_type=jnp.float32,
            )
            * scale
        )
        value_term = jnp.einsum(
            "hrk,rhd->khd",
            probs.astype(jnp.bfloat16),
            grad_heads,
            preferred_element_type=jnp.float32,
        )
        grad_key_rows, grad_value_rows = (
            lax.psum_scatter(
                key_term.reshape(group_rows, width).astype(jnp.bfloat16),
                "band",
                scatter_dimension=0,
                tiled=True,
            ).astype(jnp.float32),
            lax.psum_scatter(
                value_term.reshape(group_rows, width).astype(jnp.bfloat16),
                "band",
                scatter_dimension=0,
                tiled=True,
            ).astype(jnp.float32),
        )
        return (
            carry,
            (
                grad_query_rows.reshape(rows, width).astype(jnp.bfloat16),
                grad_key_rows.astype(jnp.bfloat16),
                grad_value_rows.astype(jnp.bfloat16),
            ),
        )

    unused, (grad_query, grad_key, grad_value) = lax.scan(
        attend_back,
        jnp.zeros((), jnp.float32),
        (
            query,
            key_back,
            value_back,
            local_seg,
            segment,
            valid,
            logsum,
            grad_attended.reshape(groups, rows, width),
        ),
    )
    grad_query = grad_query.reshape(total, width)
    grad_key = grad_key.reshape(total, width)
    grad_value = grad_value.reshape(total, width)
    grad_joined = jnp.concatenate([grad_query, grad_key, grad_value], -1)
    grad_heads_weight = jnp.einsum(
        "td,te->de", first_low, grad_joined, preferred_element_type=jnp.float32
    )
    grad_query_bias = jnp.sum(grad_query.astype(jnp.float32), 0)
    grad_value_bias = jnp.sum(grad_value.astype(jnp.float32), 0)
    grad_first = jnp.einsum(
        "te,de->td", grad_joined, heads_weight, preferred_element_type=jnp.float32
    )
    grad_start, grad_first_gain, grad_first_shift = first_back(grad_first)
    grad_start = grad_start + grad_middle
    grad_lead_weight = jnp.sum(lead_rows * grad_start, 0)
    grad_lead_bias = jnp.sum(grad_start, 0)
    (
        grad_lead_weight,
        grad_lead_bias,
        grad_first_gain,
        grad_first_shift,
        grad_heads_weight,
        grad_query_bias,
        grad_value_bias,
        grad_output,
        grad_output_bias,
        grad_second_gain,
        grad_second_shift,
        grad_up,
        grad_up_bias,
        grad_down,
        grad_down_bias,
    ) = (
        lax.psum_scatter(
            grad_lead_weight.astype(jnp.bfloat16), "band", scatter_dimension=0, tiled=True
        ).astype(jnp.float32),
        lax.psum_scatter(
            grad_lead_bias.astype(jnp.bfloat16), "band", scatter_dimension=0, tiled=True
        ).astype(jnp.float32),
        lax.psum_scatter(
            grad_first_gain.astype(jnp.bfloat16), "band", scatter_dimension=0, tiled=True
        ).astype(jnp.float32),
        lax.psum_scatter(
            grad_first_shift.astype(jnp.bfloat16), "band", scatter_dimension=0, tiled=True
        ).astype(jnp.float32),
        lax.psum_scatter(
            grad_heads_weight.astype(jnp.bfloat16), "band", scatter_dimension=0, tiled=True
        ).astype(jnp.float32),
        lax.psum_scatter(
            grad_query_bias.astype(jnp.bfloat16), "band", scatter_dimension=0, tiled=True
        ).astype(jnp.float32),
        lax.psum_scatter(
            grad_value_bias.astype(jnp.bfloat16), "band", scatter_dimension=0, tiled=True
        ).astype(jnp.float32),
        lax.psum_scatter(
            grad_output.astype(jnp.bfloat16), "band", scatter_dimension=0, tiled=True
        ).astype(jnp.float32),
        lax.psum_scatter(
            grad_output_bias.astype(jnp.bfloat16), "band", scatter_dimension=0, tiled=True
        ).astype(jnp.float32),
        lax.psum_scatter(
            grad_second_gain.astype(jnp.bfloat16), "band", scatter_dimension=0, tiled=True
        ).astype(jnp.float32),
        lax.psum_scatter(
            grad_second_shift.astype(jnp.bfloat16), "band", scatter_dimension=0, tiled=True
        ).astype(jnp.float32),
        lax.psum_scatter(
            grad_up.astype(jnp.bfloat16), "band", scatter_dimension=0, tiled=True
        ).astype(jnp.float32),
        lax.psum_scatter(
            grad_up_bias.astype(jnp.bfloat16), "band", scatter_dimension=0, tiled=True
        ).astype(jnp.float32),
        lax.psum_scatter(
            grad_down.astype(jnp.bfloat16), "band", scatter_dimension=0, tiled=True
        ).astype(jnp.float32),
        lax.psum_scatter(
            grad_down_bias.astype(jnp.bfloat16), "band", scatter_dimension=0, tiled=True
        ).astype(jnp.float32),
    )
    (
        grad_lead_weight,
        grad_lead_bias,
        grad_first_gain,
        grad_first_shift,
        grad_heads_weight,
        grad_query_bias,
        grad_value_bias,
        grad_output,
        grad_output_bias,
        grad_second_gain,
        grad_second_shift,
        grad_up,
        grad_up_bias,
        grad_down,
        grad_down_bias,
    ) = (
        lax.psum(grad_lead_weight.astype(jnp.bfloat16), "grp").astype(jnp.float32),
        lax.psum(grad_lead_bias.astype(jnp.bfloat16), "grp").astype(jnp.float32),
        lax.psum(grad_first_gain.astype(jnp.bfloat16), "grp").astype(jnp.float32),
        lax.psum(grad_first_shift.astype(jnp.bfloat16), "grp").astype(jnp.float32),
        lax.psum(grad_heads_weight.astype(jnp.bfloat16), "grp").astype(jnp.float32),
        lax.psum(grad_query_bias.astype(jnp.bfloat16), "grp").astype(jnp.float32),
        lax.psum(grad_value_bias.astype(jnp.bfloat16), "grp").astype(jnp.float32),
        lax.psum(grad_output.astype(jnp.bfloat16), "grp").astype(jnp.float32),
        lax.psum(grad_output_bias.astype(jnp.bfloat16), "grp").astype(jnp.float32),
        lax.psum(grad_second_gain.astype(jnp.bfloat16), "grp").astype(jnp.float32),
        lax.psum(grad_second_shift.astype(jnp.bfloat16), "grp").astype(jnp.float32),
        lax.psum(grad_up.astype(jnp.bfloat16), "grp").astype(jnp.float32),
        lax.psum(grad_up_bias.astype(jnp.bfloat16), "grp").astype(jnp.float32),
        lax.psum(grad_down.astype(jnp.bfloat16), "grp").astype(jnp.float32),
        lax.psum(grad_down_bias.astype(jnp.bfloat16), "grp").astype(jnp.float32),
    )
    return (
        outcome,
        grad_start.reshape(groups, rows, width),
        grad_lead_weight,
        grad_lead_bias,
        grad_first_gain,
        grad_first_shift,
        grad_heads_weight,
        grad_query_bias,
        grad_value_bias,
        grad_output,
        grad_output_bias,
        grad_second_gain,
        grad_second_shift,
        grad_up,
        grad_up_bias,
        grad_down,
        grad_down_bias,
    )


def solution(mesh):
    in_specs = (
        P("grp", "band", None),
        P("grp", None),
        P("grp", None),
        P("grp", None),
        P(),
        P(),
        P(),
        P(),
        P(),
        P(),
        P(),
        P(),
        P(),
        P(),
        P(),
        P(),
        P(),
        P(),
        P(),
        P("grp", "band", None),
    )
    out_specs = (
        P("grp", "band", None),
        P("grp", "band", None),
        P("band"),
        P("band"),
        P("band"),
        P("band"),
        P("band", None),
        P("band"),
        P("band"),
        P("band", None),
        P("band"),
        P("band"),
        P("band"),
        P("band", None),
        P("band"),
        P("band", None),
        P("band"),
    )
    return jax.shard_map(local, mesh=mesh, in_specs=in_specs, out_specs=out_specs, check_vma=False)
```

profile of v0, /device:TPU:0, one launch (start us, length us, event | category | flops | bytes accessed | tf_op | source)
XLA Modules:
  0.0 1123.4 jit_solution(8714019399420302287)
XLA Ops:
  8.3 1.3 compare_select_fusion
  9.5 1.4 fusion.32
  10.9 1.5 multiply_reduce_fusion.7
  13.0 1.3 fusion.31
  15.1 4.7 fusion.27
  20.8 2.0 copy.52
  24.7 79.0 %all-gather.5.cloned.1.call-done = bf16[2,2048,1024]{1,2,0:T(8,128)(2,1)} async-done(((bf16[2,128,1024]{1,2,0:T(8,128)(2,1)}), bf16[2,2048,1024]{1,2,0:T(8,128)(2,1)}) %all-gather.5.cloned.1.call-update) | async-done | bytes 8388624 | tf_op jit(solution)/shard_map/all_gather | solution.py:78
  103.8 79.0 %all-gather.3.cloned.1.call-done = bf16[2,2048,1024]{1,2,0:T(8,128)(2,1)} async-done(((bf16[2,128,1024]{1,2,0:T(8,128)(2,1)}), bf16[2,2048,1024]{1,2,0:T(8,128)(2,1)}) %all-gather.3.cloned.1.call-update) | async-done | bytes 8388624 | tf_op jit(solution)/shard_map/all_gather | solution.py:79
  183.7 42.6 %while.26 = (s32[]{:T(128)}, bf16[2,128,1024]{2,1,0:T(8,128)(2,1)}, f32[2,16,128,1]{2,1,3,0:T(8,128)S(1)}, bf16[2,2048,1024]{1,2,0:T(8,128)(2,1)}, s32[2,128]{1,...) while((s32[]{:T(128)}, bf16[2,128,1024]{2,1,0:T(8,128)(2,1)}, ...), condition=%wide.region_5.6_spmd, body=%wide.region_2.5_spmd.sunk | while | flops 1124728832 | bytes 95524504 | solution.py:95
  184.7 6.8 constant_dynamic-slice_fusion.20
  191.5 3.3 fusion.104
  194.8 4.4 fusion.105
  199.2 4.8 fusion.106
  205.9 6.8 constant_dynamic-slice_fusion.20
  212.7 3.3 fusion.104
  216.0 4.4 fusion.105
  220.4 4.8 fusion.106
  226.3 2.2 fusion.47
  228.9 6.4 convolution_add_fusion
  235.3 14.1 %fusion.40 = (bf16[4096]{0:T(1024)(128)(2,1)}, bf16[256,4096]{1,0:T(8,128)(2,1)S(1)}, f32[256,4096]{1,0:T(8,128)}) fusion(f32[256,4096]{1,0:T(8,128)S(1)} %convolution_add_fusion, bf16[256,1024]{1,0:T(8,128)(2,1)S(1)} %bitcast.177, bf16[4096,1024]{1,0:T(8,128)(2,1)S(1)} %bitcast.202), kind=kOutput, calls=%fused_computation.118 | convolution fusion | flops 2224025600 | bytes 19406848 | tf_op jit(solution)/shard_map/td,fd->tf/dot_general | solution.py:113
  249.4 3.2 multiply_reduce_fusion.1
  255.6 2.1 convolution_convert_fusion.3
  258.5 397.8 %while.27 = (s32[]{:T(128)}, bf16[2,128,1024]{1,2,0:T(8,128)(2,1)}, bf16[2,128,1024]{2,1,0:T(8,128)(2,1)}, bf16[2,128,1024]{1,2,0:T(8,128)(2,1)}, bf16[2,2048,10...) while((s32[]{:T(128)}, bf16[2,128,1024]{1,2,0:T(8,128)(2,1)}, ...), condition=%wide.region_14.15_spmd, body=%wide.region_10.14_spmd.sunk | while | flops 2754347008 | bytes 277182400 | solution.py:188
  259.8 4.3 constant_dynamic-slice_fusion.23
  264.1 8.1 fusion.117
  272.5 12.7 %multiply_reduce_fusion.9 = (f32[16,128]{1,0:T(8,128)S(1)}, f32[16,128,2048]{2,1,0:T(8,128)}) fusion(f32[16,128,2048]{2,1,0:T(8,128)} %fusion.117, f32[16,128]{1,0:T(8,128)S(1)} %dynamic-slice_bitcast_fusion.2, pred[128,2048]{1,0:T(8,128)(4,1)S(1)} %compare_and_fusion.5, bf16[128,16,64]{0,2,1:T(8,128)(2,1)S(1)} %bitcast.173, ...), kind=kOutput, calls=%fused_computation.20.clone.1 | convolution fusion | flops 557840384 | bytes 38289408 | tf_op jit(solution)/shard_map/while/body/eval_jaxpr/rhd,khd->hrk/dot_general | solution.py:135
  285.2 12.5 %multiply_convert_fusion.5 = bf16[16,128,2048]{2,1,0:T(8,128)(2,1)S(1)} fusion(f32[16,128,2048]{2,1,0:T(8,128)} %get-tuple-element.446, f32[16,128,2048]{2,1,0:T(8,128)} %fusion.117, f32[16,128]{1,0:T(8,128)S(1)} %get-tuple-element.447, f32[16,128]{1,0:T(8,128)S(1)} %dynamic-slice_bitcast_fusion.2, pred[128,2048]{1,0:T(8,128)(4,1)S(1)} %compare_and_fusion.5), kind=kLoop, calls=%fused_computation.19.clone.1 | loop fusion | flops 25165824 | bytes 42221568 | tf_op jit(solution)/shard_map/while/body/eval_jaxpr/convert_element_type | solution.py:140
  297.7 3.7 multiply_convert_fusion.6
  302.2 6.3 copy.83
  308.6 9.5 fusion.120
  318.1 6.5 copy.86
  324.7 8.0 fusion.119
  332.8 46.6 %reduce-scatter.23.cloned.1.call-done = bf16[128,1024]{1,0:T(8,128)(2,1)} async-done(((bf16[2048,1024]{1,0:T(8,128)(2,1)}), bf16[128,1024]{1,0:T(8,128)(2,1)}) %reduce-scatter.23.cloned.1.call-update) | async-done | bytes 262160 | tf_op jit(solution)/shard_map/while
  380.7 74.0 %reduce-scatter.25.cloned.1.call-done = bf16[128,1024]{1,0:T(8,128)(2,1)} async-done(((bf16[2048,1024]{1,0:T(8,128)(2,1)}), bf16[128,1024]{1,0:T(8,128)(2,1)}) %reduce-scatter.25.cloned.1.call-update) | async-done | bytes 262160 | tf_op jit(solution)/shard_map/while
  457.8 4.3 constant_dynamic-slice_fusion.23
  462.1 8.1 fusion.117
  470.5 12.7 %multiply_reduce_fusion.9 = (f32[16,128]{1,0:T(8,128)S(1)}, f32[16,128,2048]{2,1,0:T(8,128)}) fusion(f32[16,128,2048]{2,1,0:T(8,128)} %fusion.117, f32[16,128]{1,0:T(8,128)S(1)} %dynamic-slice_bitcast_fusion.2, pred[128,2048]{1,0:T(8,128)(4,1)S(1)} %compare_and_fusion.5, bf16[128,16,64]{0,2,1:T(8,128)(2,1)S(1)} %bitcast.173, ...), kind=kOutput, calls=%fused_computation.20.clone.1 | convolution fusion | flops 557840384 | bytes 38289408 | tf_op jit(solution)/shard_map/while/body/eval_jaxpr/rhd,khd->hrk/dot_general | solution.py:135
  483.2 12.5 %multiply_convert_fusion.5 = bf16[16,128,2048]{2,1,0:T(8,128)(2,1)S(1)} fusion(f32[16,128,2048]{2,1,0:T(8,128)} %get-tuple-element.446, f32[16,128,2048]{2,1,0:T(8,128)} %fusion.117, f32[16,128]{1,0:T(8,128)S(1)} %get-tuple-element.447, f32[16,128]{1,0:T(8,128)S(1)} %dynamic-slice_bitcast_fusion.2, pred[128,2048]{1,0:T(8,128)(4,1)S(1)} %compare_and_fusion.5), kind=kLoop, calls=%fused_computation.19.clone.1 | loop fusion | flops 25165824 | bytes 42221568 | tf_op jit(solution)/shard_map/while/body/eval_jaxpr/convert_element_type | solution.py:140
  495.8 3.7 multiply_convert_fusion.6
  500.2 6.3 copy.83
  506.6 9.3 fusion.120
  516.0 6.5 copy.86
  522.6 8.2 fusion.119
  530.8 47.8 %reduce-scatter.23.cloned.1.call-done = bf16[128,1024]{1,0:T(8,128)(2,1)} async-done(((bf16[2048,1024]{1,0:T(8,128)(2,1)}), bf16[128,1024]{1,0:T(8,128)(2,1)}) %reduce-scatter.23.cloned.1.call-update) | async-done | bytes 262160 | tf_op jit(solution)/shard_map/while
  579.9 73.9 %reduce-scatter.25.cloned.1.call-done = bf16[128,1024]{1,0:T(8,128)(2,1)} async-done(((bf16[2048,1024]{1,0:T(8,128)(2,1)}), bf16[128,1024]{1,0:T(8,128)(2,1)}) %reduce-scatter.25.cloned.1.call-update) | async-done | bytes 262160 | tf_op jit(solution)/shard_map/while
  658.5 1.4 copy.57
  660.8 4.6 convolution_convert_fusion.2
  667.4 5.7 convolution_convert_fusion.1
  673.2 4.5 multiply_convert_fusion.2
  677.7 5.6 convolution_convert_fusion
  686.5 6.6 multiply_reduce_fusion.2
  693.2 28.4 %reduce-scatter.17.cloned.1.call-done = bf16[64,1024]{1,0:T(8,128)(2,1)} async-done(((bf16[1024,1024]{1,0:T(8,128)(2,1)}), bf16[64,1024]{1,0:T(8,128)(2,1)}) %reduce-scatter.17.cloned.1.call-update) | async-done | bytes 131088 | tf_op jit(solution)/shard_map/reduce_scatter | solution.py:256
  721.6 88.7 %reduce-scatter.15.cloned.1.call-done = bf16[64,3072]{1,0:T(8,128)(2,1)} async-done(((bf16[1024,3072]{1,0:T(8,128)(2,1)}), bf16[64,3072]{1,0:T(8,128)(2,1)}) %reduce-scatter.15.cloned.1.call-update) | async-done | bytes 393232 | tf_op jit(solution)/shard_map/reduce_scatter | solution.py:247
  810.3 108.0 %reduce-scatter.19.cloned.1.call-done = bf16[64,4096]{1,0:T(8,128)(2,1)} async-done(((bf16[1024,4096]{1,0:T(8,128)(2,1)}), bf16[64,4096]{1,0:T(8,128)(2,1)}) %reduce-scatter.19.cloned.1.call-update) | async-done | bytes 524304 | tf_op jit(solution)/shard_map/reduce_scatter | solution.py:268
  918.3 108.3 %reduce-scatter.21.cloned.1.call-done = bf16[256,1024]{1,0:T(8,128)(2,1)} async-done(((bf16[4096,1024]{1,0:T(8,128)(2,1)}), bf16[256,1024]{1,0:T(8,128)(2,1)}) %reduce-scatter.21.cloned.1.call-update) | async-done | bytes 524304 | tf_op jit(solution)/shard_map/reduce_scatter | solution.py:274
  1026.6 1.8 fusion.44
  1028.5 1.3 fusion.39
  1029.8 60.3 %all-reduce.11 = (bf16[1024]{0:T(1024)(128)(2,1)S(1)}, bf16[1024]{0:T(1024)(128)(2,1)S(1)}, bf16[1024]{0:T(1024)(128)(2,1)S(1)}, bf16[1024]{0:T(1024)(128)(2,1)S...) all-reduce(bf16[1024]{0:T(1024)(128)(2,1)S(1)} %get-tuple-element.2, ...), channel_id=4, replica_groups=mesh['band'=16,'grp'=2] {'band'}, use_global_device_ids=true, to_apply=%region_18.19.clone | all-reduce | flops 14336 | bytes 57344
  1090.9 5.0 all-reduce.12
  1101.6 7.3 fusion.30
  1108.9 1.6 convert_element_type.243
  1110.5 1.9 convert_element_type.239
  1112.4 2.1 convert_element_type.250
  1114.5 2.1 convert_element_type.253
  (272 shorter events, 38.2 us)
Async XLA Ops:
  7.2 219.1 %copy-start = (bf16[1024,1024]{1,0:T(8,128)(2,1)S(1)}, bf16[1024,1024]{1,0:T(8,128)(2,1)}, u32[]{:S(2)}) copy-start(bf16[1024,1024]{1,0:T(8,128)(2,1)} %param.35) | copy-start | bytes 6291460
  7.2 96.6 %all-gather.5.cloned.1.call-start = ((), (), s32[]{:S(2)}) async-start(), calls=%async_computation.7 | async-start | bytes 8912896 | tf_op jit(solution)/shard_map/all_gather | solution.py:78
  9.5 5.6 copy-start.39
  10.9 8.9 copy-start.53
  13.0 6.8 copy-start.55
  14.2 5.6 copy-start.16
  19.8 163.8 %copy-start.31 = (s32[2,2048]{1,0:T(2,128)S(1)}, s32[2,2048]{1,0:T(2,128)}, u32[]{:S(2)}) copy-start(s32[2,2048]{1,0:T(2,128)} %param.26) | copy-start | bytes 49156
  19.8 163.8 %copy-start.32 = (s32[2,2048]{1,0:T(2,128)S(1)}, s32[2,2048]{1,0:T(2,128)}, u32[]{:S(2)}) copy-start(s32[2,2048]{1,0:T(2,128)} %param.27) | copy-start | bytes 49156
  22.8 160.0 %all-gather.3.cloned.1.call-start = ((), (), s32[]{:S(2)}) async-start(), calls=%async_computation.6 | async-start | bytes 8912896 | tf_op jit(solution)/shard_map/all_gather | solution.py:79
  183.7 42.6 %copy-start.45 = (f32[1024]{0:T(1024)S(1)}, f32[1024]{0:T(1024)}, u32[]{:S(2)}) copy-start(f32[1024]{0:T(1024)} %param.36) | copy-start | bytes 12292
  194.8 4.4 copy-start.4
  216.0 4.4 copy-start.4
  228.5 24.1 %copy-start.5 = (f32[256,1024]{1,0:T(8,128)}, f32[256,1024]{1,0:T(8,128)S(1)}, u32[]{:S(2)}) copy-start(f32[256,1024]{1,0:T(8,128)S(1)} %get-tuple-element.301) | copy-start | bytes 3145732
  228.5 24.1 %copy-start.41 = (f32[256]{0:T(256)}, f32[256]{0:T(256)S(1)}, u32[]{:S(2)}) copy-start(f32[256]{0:T(256)S(1)} %broadcast_multiply_fusion) | copy-start | bytes 3076
  228.5 6.7 slice-start.2
  228.8 23.8 %copy-start.43 = (f32[256]{0:T(256)}, f32[256]{0:T(256)S(1)}, u32[]{:S(2)}) copy-start(f32[256]{0:T(256)S(1)} %fusion.35) | copy-start | bytes 3076
  228.8 6.4 copy-start.10
  228.8 6.4 slice-start.3
  228.9 20.5 %slice-start = ((s8[8388608]{0:T(1024)(128)(4,1)}), s8[4194304]{0:T(1024)(128)(4,1)S(1)}, s32[]{:S(2)}) async-start(s8[8388608]{0:T(1024)(128)(4,1)} %bitcast.199), calls=%async_computation.15 | async-start | bytes 8388608
  235.2 14.1 %copy-start.15 = (f32[256,4096]{1,0:T(8,128)}, f32[256,4096]{1,0:T(8,128)S(1)}, u32[]{:S(2)}) copy-start(f32[256,4096]{1,0:T(8,128)S(1)} %convolution_add_fusion) | copy-start | bytes 12582916
  235.3 14.1 %slice-start.1 = ((s8[8388608]{0:T(1024)(128)(4,1)}), s8[4194304]{0:T(1024)(128)(4,1)S(1)}, s32[]{:S(2)}) async-start(s8[8388608]{0:T(1024)(128)(4,1)} %bitcast.199), calls=%async_computation.16 | async-start | bytes 8388608
  249.4 3.2 copy-start.18
  253.0 4.6 copy-start.46
  258.7 120.7 %reduce-scatter.23.cloned.1.call-start = ((), (), s32[]{:S(2)}) async-start(), calls=%async_computation.13 | async-start | bytes 4456448 | tf_op jit(solution)/shard_map/while
  264.1 8.1 copy-start.3
  297.7 4.5 copy-start.2
  308.6 146.1 %reduce-scatter.25.cloned.1.call-start = ((), (), s32[]{:S(2)}) async-start(), calls=%async_computation.14 | async-start | bytes 4456448 | tf_op jit(solution)/shard_map/while
  324.7 8.1 copy-start.23
  324.7 131.1 %copy-start.20 = (bf16[2,128,1024]{1,2,0:T(8,128)(2,1)S(1)}, bf16[2,128,1024]{1,2,0:T(8,128)(2,1)}, u32[]{:S(2)}) copy-start(bf16[2,128,1024]{1,2,0:T(8,128)(2,1)} %get-tuple-element.494) | copy-start | bytes 1572868 | tf_op jit(solution)/shard_map/while
  324.7 131.2 %copy-start.26 = (bf16[2,128,1024]{2,1,0:T(8,128)(2,1)S(1)}, bf16[2,128,1024]{2,1,0:T(8,128)(2,1)}, u32[]{:S(2)}) copy-start(bf16[2,128,1024]{2,1,0:T(8,128)(2,1)} %get-tuple-element.493) | copy-start | bytes 1572868 | tf_op jit(solution)/shard_map/while
  332.8 123.1 %copy-start.24 = (bf16[2,128,1024]{1,2,0:T(8,128)(2,1)}, bf16[2,128,1024]{1,2,0:T(8,128)(2,1)S(1)}, u32[]{:S(2)}) copy-start(bf16[2,128,1024]{1,2,0:T(8,128)(2,1)S(1)} %constant_dynamic-update-slice_fusion.7) | copy-start | bytes 1572868 | tf_op jit(solution)/shard_map/while
  456.8 121.8 %reduce-scatter.23.cloned.1.call-start = ((), (), s32[]{:S(2)}) async-start(), calls=%async_computation.13 | async-start | bytes 4456448 | tf_op jit(solution)/shard_map/while
  462.1 8.1 copy-start.3
  495.8 4.5 copy-start.2
  506.6 147.2 %reduce-scatter.25.cloned.1.call-start = ((), (), s32[]{:S(2)}) async-start(), calls=%async_computation.14 | async-start | bytes 4456448 | tf_op jit(solution)/shard_map/while
  522.5 8.2 copy-start.23
  522.5 132.4 %copy-start.20 = (bf16[2,128,1024]{1,2,0:T(8,128)(2,1)S(1)}, bf16[2,128,1024]{1,2,0:T(8,128)(2,1)}, u32[]{:S(2)}) copy-start(bf16[2,128,1024]{1,2,0:T(8,128)(2,1)} %get-tuple-element.494) | copy-start | bytes 1572868 | tf_op jit(solution)/shard_map/while
  522.5 132.4 %copy-start.26 = (bf16[2,128,1024]{2,1,0:T(8,128)(2,1)S(1)}, bf16[2,128,1024]{2,1,0:T(8,128)(2,1)}, u32[]{:S(2)}) copy-start(bf16[2,128,1024]{2,1,0:T(8,128)(2,1)} %get-tuple-element.493) | copy-start | bytes 1572868 | tf_op jit(solution)/shard_map/while
  530.8 124.2 %copy-start.24 = (bf16[2,128,1024]{1,2,0:T(8,128)(2,1)}, bf16[2,128,1024]{1,2,0:T(8,128)(2,1)S(1)}, u32[]{:S(2)}) copy-start(bf16[2,128,1024]{1,2,0:T(8,128)(2,1)S(1)} %constant_dynamic-update-slice_fusion.7) | copy-start | bytes 1572868 | tf_op jit(solution)/shard_map/while
  656.3 4.4 copy-start.17
  656.4 4.4 copy-start.28
  656.4 4.4 copy-start.52
  656.4 4.4 copy-start.54
  656.4 4.4 copy-start.56
  656.4 4.4 copy-start.60
  656.4 65.2 %reduce-scatter.17.cloned.1.call-start = ((), (), s32[]{:S(2)}) async-start(), calls=%async_computation.9 | async-start | bytes 2228224 | tf_op jit(solution)/shard_map/reduce_scatter | solution.py:256
  657.2 153.2 %reduce-scatter.15.cloned.1.call-start = ((), (), s32[]{:S(2)}) async-start(), calls=%async_computation.8 | async-start | bytes 6684672 | tf_op jit(solution)/shard_map/reduce_scatter | solution.py:247
  665.5 252.8 %reduce-scatter.19.cloned.1.call-start = ((), (), s32[]{:S(2)}) async-start(), calls=%async_computation.10 | async-start | bytes 8912896 | tf_op jit(solution)/shard_map/reduce_scatter | solution.py:268
  673.1 353.4 %reduce-scatter.21.cloned.1.call-start = ((), (), s32[]{:S(2)}) async-start(), calls=%async_computation.11 | async-start | bytes 8912896 | tf_op jit(solution)/shard_map/reduce_scatter | solution.py:274
  673.2 4.5 copy-start.11
  677.7 5.6 copy-start.7
  683.3 3.1 copy-start.13
  683.4 3.1 copy-start.37
  683.4 3.1 copy-start.38
  683.4 425.5 %all-reduce.16.cloned.1.call-start = ((), (), s32[]{:S(2)}) async-start(), calls=%async_computation.12 | async-start | bytes 3145728 | tf_op jit(solution)/shard_map/psum | solution.py:302
  686.5 6.7 copy-start.49
  693.1 335.4 %copy-start.9 = (f32[256,1024]{1,0:T(8,128)S(1)}, f32[256,1024]{1,0:T(8,128)}, u32[]{:S(2)}) copy-start(f32[256,1024]{1,0:T(8,128)} %copy-done.8) | copy-start | bytes 3145732
  693.1 335.4 %copy-start.47 = (f32[256]{0:T(256)S(1)}, f32[256]{0:T(256)}, u32[]{:S(2)}) copy-start(f32[256]{0:T(256)} %copy-done.46) | copy-start | bytes 3076
  693.1 336.7 %copy-start.50 = (bf16[1024]{0:T(1024)(128)(2,1)S(1)}, bf16[1024]{0:T(1024)(128)(2,1)}, u32[]{:S(2)}) copy-start(bf16[1024]{0:T(1024)(128)(2,1)} %get-tuple-element.278) | copy-start | bytes 6148
  693.1 336.7 %copy-start.51 = (bf16[4096]{0:T(1024)(128)(2,1)S(1)}, bf16[4096]{0:T(1024)(128)(2,1)}, u32[]{:S(2)}) copy-start(bf16[4096]{0:T(1024)(128)(2,1)} %get-tuple-element.275) | copy-start | bytes 24580
  693.1 336.7 %copy-start.57 = (bf16[1024]{0:T(1024)(128)(2,1)S(1)}, bf16[1024]{0:T(1024)(128)(2,1)}, u32[]{:S(2)}) copy-start(bf16[1024]{0:T(1024)(128)(2,1)} %get-tuple-element.197) | copy-start | bytes 6148
  693.1 336.7 %copy-start.58 = (bf16[1024]{0:T(1024)(128)(2,1)S(1)}, bf16[1024]{0:T(1024)(128)(2,1)}, u32[]{:S(2)}) copy-start(bf16[1024]{0:T(1024)(128)(2,1)} %get-tuple-element.201) | copy-start | bytes 6148
  693.1 408.5 %copy-start.61 = (f32[1024]{0:T(1024)S(1)}, f32[1024]{0:T(1024)}, u32[]{:S(2)}) copy-start(f32[1024]{0:T(1024)} %param.42) | copy-start | bytes 12292
  1101.6 15.1 %copy-start.1 = (bf16[1024,1024]{1,0:T(8,128)(2,1)S(1)}, bf16[1024,1024]{1,0:T(8,128)(2,1)}, u32[]{:S(2)}) copy-start(bf16[1024,1024]{1,0:T(8,128)(2,1)} %param.35) | copy-start | bytes 6291460
  (23 other events, 40.7 us)
Sparse Core Ops, SparseCore 0:
  22.9 80.7 all-gather.4
  106.5 76.2 all-gather.2
  308.7 70.6 reduce-scatter.22
  383.1 71.5 reduce-scatter.24
  506.7 71.8 reduce-scatter.22
  582.3 71.4 reduce-scatter.24
  661.0 60.5 reduce-scatter.16
  726.0 84.2 reduce-scatter.14
  814.4 103.8 reduce-scatter.18
  922.2 104.3 reduce-scatter.20
  1029.1 51.7 all-reduce.15
where the time goes:
time: 1130 us; the launch traced here: 1120 us
  waiting for transfers between devices  735 us (65%)
  matrix products  163 us (14%)
  local copies, waits for them, and re-layouts  76.3 us (7%)
  blocking collectives  65.2 us (6%)
  other arithmetic  65.1 us (6%)
  between operations  16.1 us (1%)
    while x8, waiting for transfers between devices  242 us
    reduce_scatter x1, waiting for transfers between devices, local(): lax.psum_scatter(grad_down.astype(jnp.bfloat16), 'band', scatter_dimensio...  108 us
    reduce_scatter x1, waiting for transfers between devices, local(): lax.psum_scatter(grad_up.astype(jnp.bfloat16), 'band', scatter_dimension=...  108 us
    reduce_scatter x1, waiting for transfers between devices, local(): lax.psum_scatter(grad_heads_weight.astype(jnp.bfloat16), 'band', scatter_...  88.7 us
    all_gather x1, waiting for transfers between devices, local(): lax.all_gather(local_keys, 'band', axis=1, tiled=True)  79 us
    all_gather x1, waiting for transfers between devices, local(): lax.all_gather(local_values, 'band', axis=1, tiled=True)  79 us
    unnamed x1, blocking collectives  60.3 us
    while x44, local copies, waits for them, and re-layouts  33.6 us
  transfers between devices with their start and end apart: 11, of which 10 were waited for; matrix products, arithmetic and copies ran while one was open for 9% of the time, Pallas kernels for 0%

commit v1 on v0

v1 whole, which is shorter than its diff:
```python
import functools

import jax
import jax.numpy as jnp
from jax import lax
from jax.experimental import pallas as pl
from jax.experimental.pallas import tpu as pltpu
from jax.sharding import PartitionSpec as P

HEADS = 16
HEAD_DIM = 64
LANES = 128
MESH = pl.DeviceIdType.MESH
F32 = jnp.float32
BF16 = jnp.bfloat16
VMEM_BYTES = 56 * 2**20
MASKED = -1e30


def layer_norm(values, gain, shift):
    center = values - jnp.mean(values, -1, keepdims=True)
    spread = jnp.mean(center * center, -1, keepdims=True)
    return center * lax.rsqrt(spread + 1e-05) * gain + shift


def gelu_exact(values):
    return jax.nn.gelu(values, approximate=False)


def lane_of(shape):
    return lax.broadcasted_iota(jnp.int32, shape, 1)


def in_head(shape, head):
    return lane_of(shape) // HEAD_DIM == head


def spare_lane(shape, head):
    lane = lane_of(shape)
    return jnp.where(lane // HEAD_DIM == head, LANES, lane % HEAD_DIM)


def split_terms(column, spare):
    high = column.astype(BF16).astype(F32)
    middle = (column - high).astype(BF16).astype(F32)
    low = column - high - middle
    return (
        jnp.where(spare == 2, high, 0.0)
        + jnp.where(spare == 3, middle, 0.0)
        + jnp.where(spare == 4, low, 0.0)
    )


def dot_nt(left, right):
    return lax.dot_general(left, right, (((1,), (1,)), ((), ())), preferred_element_type=F32)


def dot_tn(left, right):
    return lax.dot_general(left, right, (((0,), (0,)), ((), ())), preferred_element_type=F32)


def dot_nn(left, right):
    return jnp.dot(left, right, preferred_element_type=F32)


def forward_kernel(
    block, members, pairs,
    blocks_ref, query_aux_ref, key_aux_ref,
    qkv_ref, attended_ref, out_full_ref, query_ref,
    qkv_in, key_s, value_s, out_s,
    local_sem, keep_sem, qkv_send, qkv_recv, out_send, out_recv,
):
    rows = members * block
    scale = HEAD_DIM ** (-0.5)
    copies = members // pairs
    band, grp = lax.axis_index("band"), lax.axis_index("grp")
    me = lax.rem(band, members)
    base = band - me
    others = [lax.rem(me + i, members) for i in range(1, members)]

    barrier = pltpu.get_barrier_semaphore()
    for other in others:
        pl.semaphore_signal(barrier, inc=1, device_id=(base + other, grp), device_id_type=MESH)
    pl.semaphore_wait(barrier, len(others))

    def remote(source, target, send, recv, device):
        return pltpu.make_async_remote_copy(
            src_ref=source, dst_ref=target, send_sem=send, recv_sem=recv, device_id=device, device_id_type=MESH
        )

    qkv_copies = {}
    for t in (1, 2, 0):
        for i, other in enumerate(others):
            qkv_copies[t, i] = remote(
                blocks_ref.at[other // copies, t],
                qkv_in.at[me, t],
                qkv_send.at[t, i],
                qkv_recv.at[t, i],
                (base + other, grp),
            )
            qkv_copies[t, i].start()
    own = pltpu.make_async_copy(blocks_ref.at[me // copies], qkv_in.at[me], local_sem)
    own.start()
    own.wait()
    for i in range(members - 1):
        qkv_copies[1, i].wait_recv()
    keys = qkv_in[:, 1].reshape(rows, LANES)
    for head in range(2):
        key_s[head] = jnp.where(in_head(keys.shape, head), keys, key_aux_ref[...])
    for i in range(members - 1):
        qkv_copies[2, i].wait_recv()
    value_s[...] = qkv_in[:, 2].reshape(rows, LANES)

    def sends_to(other):
        return (lax.rem(other, copies) == lax.rem(me, copies)) & (other != me)

    def out_copy(other):
        return remote(
            out_s.at[other],
            attended_ref.at[me // copies],
            out_send.at[other // copies],
            out_recv.at[me // copies],
            (base + other, grp),
        )

    @pl.loop(0, members)
    def _(i):
        other = lax.rem(me + members - i, members)

        @pl.when(i > 0)
        def _():
            pltpu.make_async_copy(qkv_in.at[other, 0], qkv_in.at[other, 0], qkv_recv.at[0, i - 1]).wait()

        here = pl.ds(pl.multiple_of(other * block, block), block)
        query = qkv_in[other, 0].astype(F32) * scale
        aux = query_aux_ref[here].astype(F32)
        shape = query.shape
        mixed = []
        for head in range(2):
            inside = in_head(shape, head)
            marked = jnp.where(inside, query, aux)
            scores = dot_nt(marked.astype(BF16), key_s[head])
            peak = jnp.max(scores, -1, keepdims=True)
            weights = jnp.exp(scores - peak)
            total = jnp.sum(weights, -1, keepdims=True)
            mixed.append(dot_nn(weights.astype(BF16), value_s[...]) / total)
            logsum = peak + jnp.log(total)
            marked = marked + split_terms(-logsum, spare_lane(shape, head))
            query_ref[head, here] = marked.astype(BF16)
        both = jnp.where(in_head(shape, 0), mixed[0], mixed[1])
        out_full_ref[here] = both
        out_s[other, 0] = both.astype(BF16)

        @pl.when(sends_to(other))
        def _():
            out_copy(other).start()

    keep = pltpu.make_async_copy(qkv_in, qkv_ref, keep_sem)
    keep.start()
    own_out = pltpu.make_async_copy(out_s.at[me], attended_ref.at[me // copies], local_sem)
    own_out.start()
    keep.wait()
    own_out.wait()
    for copy in qkv_copies.values():
        copy.wait_send()
    for other in others:

        @pl.when(sends_to(other))
        def _():
            out_copy(other).wait_send()

    for i in range(1, pairs):
        slot = lax.rem(me // copies + i, pairs)
        pltpu.make_async_copy(attended_ref.at[slot], attended_ref.at[slot], out_recv.at[slot]).wait()


def attention_forward(blocks, query_aux, key_aux, members, collective_id):
    pairs, _, block, _ = blocks.shape
    rows = members * block
    vmem = pl.BlockSpec(memory_space=pltpu.VMEM)
    anywhere = pl.BlockSpec(memory_space=pl.ANY)
    dma = pltpu.SemaphoreType.DMA
    return pl.pallas_call(
        functools.partial(forward_kernel, block, members, pairs),
        out_shape=(
            jax.ShapeDtypeStruct((members, 3, block, LANES), BF16),
            jax.ShapeDtypeStruct((pairs, 1, block, LANES), BF16),
            jax.ShapeDtypeStruct((rows, LANES), F32),
            jax.ShapeDtypeStruct((2, rows, LANES), BF16),
        ),
        in_specs=[anywhere, vmem, vmem],
        out_specs=(anywhere, anywhere, vmem, vmem),
        scratch_shapes=[
            pltpu.VMEM((members, 3, block, LANES), BF16),
            pltpu.VMEM((2, rows, LANES), BF16),
            pltpu.VMEM((rows, LANES), BF16),
            pltpu.VMEM((members, 1, block, LANES), BF16),
            dma, dma, dma((3, members)), dma((3, members)), dma((members,)), dma((members,)),
        ],
        compiler_params=pltpu.CompilerParams(
            vmem_limit_bytes=VMEM_BYTES, collective_id=collective_id, has_side_effects=True
        ),
        cost_estimate=pl.CostEstimate(
            flops=8 * rows * rows * LANES, bytes_accessed=32 * 2**20, transcendentals=2 * rows * rows
        ),
        name="attention_forward",
    )(blocks, query_aux, key_aux)


def device_at(axis, index):
    band, grp = lax.axis_index("band"), lax.axis_index("grp")
    return (index, grp) if axis == "band" else (band, index)


def flip(axis, bit):
    index = lax.axis_index(axis)
    mine = lax.rem(index // (1 << bit), 2)
    return mine, device_at(axis, index + (1 - 2 * mine) * (1 << bit))


def normalised(values):
    center = values - jnp.mean(values, -1, keepdims=True)
    spread = jnp.mean(center * center, -1, keepdims=True)
    inverse = lax.rsqrt(spread + 1e-05)
    return center * inverse, inverse


def norm_backward(grads, gain, unit, inverse):
    inner = grads * gain
    at_input = inverse * (
        inner
        - jnp.mean(inner, -1, keepdims=True)
        - unit * jnp.mean(inner * unit, -1, keepdims=True)
    )
    return at_input, jnp.sum(grads * unit, 0, keepdims=True), jnp.sum(grads, 0, keepdims=True)


def by_core(value, core, held, away_ref, stay_ref):
    split = value.astype(BF16).reshape(-1, 2, held, value.shape[-1])
    even, odd = split[:, 0], split[:, 1]
    away_ref[...] = jnp.where(core == 0, odd, even)
    stay_ref[...] = jnp.where(core == 0, even, odd)


def heads_kernel(
    tokens_ref, lead_ref, lead_weight_ref, lead_bias_ref, gain_ref, shift_ref, weight_ref, bias_ref,
    start_ref, first_ref, out_ref,
):
    part = pl.program_id(0)

    @pl.when(part == 0)
    def _():
        start = tokens_ref[...].astype(F32) + lead_ref[...] * lead_weight_ref[...] + lead_bias_ref[...]
        start_ref[...] = start
        first_ref[...] = (normalised(start)[0] * gain_ref[...] + shift_ref[...]).astype(BF16)

    joined = (dot_nn(first_ref[...], weight_ref[...]) + bias_ref[0]).astype(BF16)
    for pair in range(out_ref.shape[0]):
        out_ref[pair, 0] = joined[:, pair * LANES : (pair + 1) * LANES]


def constant(*shape):
    return pl.BlockSpec(shape, lambda *i: (0,) * len(shape))


def heads_forward(tokens, lead_rows, lead_weight, lead_bias, gain, shift, weight, bias):
    total, width = tokens.shape
    pairs = width // LANES
    row = lambda v: v.reshape(1, width)
    return pl.pallas_call(
        heads_kernel,
        grid=(3,),
        out_shape=(
            jax.ShapeDtypeStruct((total, width), F32),
            jax.ShapeDtypeStruct((total, width), BF16),
            jax.ShapeDtypeStruct((pairs, 3, total, LANES), BF16),
        ),
        in_specs=[constant(total, width), constant(total, 1)]
        + [constant(1, width)] * 4
        + [
            pl.BlockSpec((width, width), lambda i: (0, i)),
            pl.BlockSpec((1, 1, width), lambda i: (i, 0, 0)),
        ],
        out_specs=(
            constant(total, width),
            constant(total, width),
            pl.BlockSpec((pairs, 1, total, LANES), lambda i: (0, i, 0, 0)),
        ),
        compiler_params=pltpu.CompilerParams(vmem_limit_bytes=VMEM_BYTES),
        cost_estimate=pl.CostEstimate(
            flops=6 * total * width * width, bytes_accessed=6 * width * width, transcendentals=0
        ),
        name="heads_forward",
    )(tokens, lead_rows, row(lead_weight), row(lead_bias), row(gain), row(shift), weight, bias)


def feed_kernel(
    core_ref, attended_ref, start_ref, grad_ref, output_weight_ref, output_bias_ref, gain_ref, shift_ref,
    up_ref, up_bias_ref, down_ref, down_bias_ref,
    result_ref, grad_middle_ref, grad_attended_ref, down_away, down_stay, up_away, up_stay,
    output_away, output_stay, vectors_ref, up_vector_ref,
    attended_s, middle_s, unit_s, inverse_s, second_s, second_turned, result_s, grad_second_s,
):
    step, steps = pl.program_id(0), pl.num_programs(0)
    core = core_ref[0]
    pairs = attended_ref.shape[0]

    @pl.when(step == 0)
    def _():
        for pair in range(pairs):
            attended_s[:, pair * LANES : (pair + 1) * LANES] = attended_ref[pair, 0]
        middle = (
            start_ref[...] + dot_nn(attended_s[...], output_weight_ref[...]) + output_bias_ref[...]
        )
        middle_s[...] = middle
        unit, inverse = normalised(middle)
        unit_s[...] = unit
        inverse_s[...] = inverse
        second = unit * gain_ref[...] + shift_ref[...]
        second_s[...] = second.astype(BF16)
        second_turned[...] = second.T.astype(BF16)
        result_s[...] = jnp.zeros_like(result_s)
        grad_second_s[...] = jnp.zeros_like(grad_second_s)

    grads = grad_ref[...]
    upper = dot_nn(second_s[...], up_ref[...]) + up_bias_ref[...]
    level = 0.5 + 0.5 * lax.erf(upper * 0.7071067811865476)
    hidden = (upper * level).astype(BF16)
    slope = level + upper * (0.3989422804014327 * jnp.exp(-0.5 * upper * upper))
    result_s[...] += dot_nn(hidden, down_ref[...])
    by_core(dot_tn(hidden, grads), core, down_away.shape[1], down_away, down_stay)
    grad_upper_wide = dot_nt(grads, down_ref[...]) * slope
    grad_upper = grad_upper_wide.astype(BF16)
    up_vector_ref[...] = jnp.sum(grad_upper.astype(F32), 0, keepdims=True)
    by_core(dot_nn(second_turned[...], grad_upper), core, up_away.shape[1], up_away, up_stay)
    grad_second_s[...] += dot_nt(grad_upper, up_ref[...])

    @pl.when(step == steps - 1)
    def _():
        result_ref[...] = (middle_s[...] + result_s[...] + down_bias_ref[...]).astype(BF16)
        wide = grads.astype(F32)
        at_input, grad_gain, grad_shift = norm_backward(
            grad_second_s[...], gain_ref[...], unit_s[...], inverse_s[...]
        )
        grad_middle = at_input + wide
        grad_middle_ref[...] = grad_middle
        branch = grad_middle.astype(BF16)
        by_core(dot_tn(attended_s[...], branch), core, output_away.shape[1], output_away, output_stay)
        grad_attended = dot_nt(branch, output_weight_ref[...]).astype(BF16)
        for pair in range(pairs):
            grad_attended_ref[pair, 0] = grad_attended[:, pair * LANES : (pair + 1) * LANES]
        vectors_ref[0:1] = jnp.sum(branch.astype(F32), 0, keepdims=True)
        vectors_ref[1:2] = grad_gain
        vectors_ref[2:3] = grad_shift
        vectors_ref[3:4] = jnp.sum(wide, 0, keepdims=True)


def feed(core, attended, start, grads, output_weight, output_bias, gain, shift, up, up_bias, down, down_bias, bands):
    total, width = start.shape
    inner = up.shape[1]
    pairs = width // LANES
    chunk = 512
    held, held_down = width // bands, inner // bands
    per_chunk = chunk // held_down // 2
    row = lambda v: v.reshape(1, -1)
    half = bands // 2
    one = lambda *shape: constant(*shape)
    return pl.pallas_call(
        feed_kernel,
        grid_spec=pltpu.PrefetchScalarGridSpec(
            num_scalar_prefetch=1,
            grid=(inner // chunk,),
            in_specs=[
                one(pairs, 1, total, LANES),
                one(total, width),
                one(total, width),
                one(width, width),
                one(1, width),
                one(1, width),
                one(1, width),
                pl.BlockSpec((width, chunk), lambda j, c: (0, j)),
                pl.BlockSpec((1, chunk), lambda j, c: (0, j)),
                pl.BlockSpec((chunk, width), lambda j, c: (j, 0)),
                one(1, width),
            ],
            out_specs=(
                one(total, width),
                one(total, width),
                one(pairs, 1, total, LANES),
                pl.BlockSpec((per_chunk, held_down, width), lambda j, c: (j, 0, 0)),
                pl.BlockSpec((per_chunk, held_down, width), lambda j, c: (j, 0, 0)),
                pl.BlockSpec((half, held, chunk), lambda j, c: (0, 0, j)),
                pl.BlockSpec((half, held, chunk), lambda j, c: (0, 0, j)),
                one(half, held, width),
                one(half, held, width),
                one(8, width),
                pl.BlockSpec((1, chunk), lambda j, c: (0, j)),
            ),
            scratch_shapes=[
                pltpu.VMEM((total, width), BF16),
                pltpu.VMEM((total, width), F32),
                pltpu.VMEM((total, width), F32),
                pltpu.VMEM((total, 1), F32),
                pltpu.VMEM((total, width), BF16),
                pltpu.VMEM((width, total), BF16),
                pltpu.VMEM((total, width), F32),
                pltpu.VMEM((total, width), F32),
            ],
        ),
        out_shape=(
            jax.ShapeDtypeStruct((total, width), BF16),
            jax.ShapeDtypeStruct((total, width), F32),
            jax.ShapeDtypeStruct((pairs, 1, total, LANES), BF16),
            jax.ShapeDtypeStruct((half, held_down, width), BF16),
            jax.ShapeDtypeStruct((half, held_down, width), BF16),
            jax.ShapeDtypeStruct((half, held, inner), BF16),
            jax.ShapeDtypeStruct((half, held, inner), BF16),
            jax.ShapeDtypeStruct((half, held, width), BF16),
            jax.ShapeDtypeStruct((half, held, width), BF16),
            jax.ShapeDtypeStruct((8, width), F32),
            jax.ShapeDtypeStruct((1, inner), F32),
        ),
        compiler_params=pltpu.CompilerParams(vmem_limit_bytes=VMEM_BYTES),
        cost_estimate=pl.CostEstimate(
            flops=12 * total * width * inner, bytes_accessed=8 * width * inner, transcendentals=2 * total * inner
        ),
        name="feed",
    )(
        core, attended, start, grads, output_weight, row(output_bias), row(gain), row(shift),
        up, row(up_bias), down, row(down_bias),
    )


LINK = 22.3
CORE = 1.5
ADD = 0.35
HOP = 1.5


def plan_events(parts, tasks):
    free, waiting, slots, now = {}, [], [[] for _ in range(len(tasks) + 1)], 0.0
    ready = 3.0
    for k, (size, links) in enumerate(parts):
        ready += size * CORE
        waiting.append((ready, k, size, list(links)))
    for slot in range(len(tasks) + 1):
        while waiting:
            waiting.sort()
            if slot < len(tasks) and waiting[0][0] > now:
                break
            arrival, k, size, links = waiting.pop(0)
            now = max(now, arrival) + size * ADD
            slots[slot].append(k)
            if links:
                link = links.pop(0)
                size /= 2
                begin = max(now, free.get(link, 0.0))
                if link == "Z":
                    end = begin + 2 * size * LINK
                    free["z"] = max(free.get("z", 0.0), now) + size * LINK
                else:
                    end = begin + size * LINK
                free[link] = end
                waiting.append((end + HOP, k, size, links))
            else:
                free["y"] = max(now, free.get("y", 0.0)) + size * LINK
        if slot < len(tasks):
            now += tasks[slot]
    return slots


class Flow:
    def __init__(self, k, plan, away, stay, core_in, stay_s, buffers, sems):
        self.k, self.plan, self.away, self.stay = k, plan, away, stay
        self.core_in, self.stay_s, self.buffers = core_in, stay_s, buffers
        self.core_send, self.core_recv, self.stay_sem, self.send_sem, self.recv_sem = sems
        self.stages, self.lead = plan["stages"], list(plan["lead"])
        self.flips = [flip(*stage) for stage in self.stages]
        self.core_other = flip("band", 0)[1]
        self.held, self.at = None, -1

    @staticmethod
    def shapes(plan):
        shape, lead = [2] * len(plan["lead"]) + [plan["rows"][1], plan["columns"][1]], list(plan["lead"])
        found = [tuple(shape)]
        for axis, bit in plan["stages"]:
            if axis == "band":
                at = lead.index(bit)
                del shape[at], lead[at]
            else:
                shape[-1] //= 2
            found.append(tuple(shape))
        return found

    def region(self, stage, index):
        (first, rows), (column, columns) = self.plan["rows"], self.plan["columns"]
        where = [slice(None)] * len(self.plan["lead"]) + [pl.ds(first, rows), pl.ds(column, columns)]
        if stage is not None:
            axis, bit = stage
            if axis == "band":
                where[self.plan["lead"].index(bit)] = index
            else:
                half = columns // 2
                where[-1] = pl.ds(pl.multiple_of(column + index * half, LANES), half)
        return tuple(where)

    def pick(self, ref, index):
        axis, bit = self.stages[self.at]
        where = [slice(None)] * len(ref.shape)
        if axis == "band":
            where[self.lead.index(bit)] = index
        else:
            half = ref.shape[-1] // 2
            where[-1] = pl.ds(pl.multiple_of(index * half, LANES), half)
        return tuple(where)

    def core_copy(self):
        return pltpu.make_async_remote_copy(
            src_ref=self.away.at[self.region(None, None)],
            dst_ref=self.core_in,
            send_sem=self.core_send.at[self.k],
            recv_sem=self.core_recv.at[self.k],
            device_id=self.core_other,
            device_id_type=MESH,
        )

    def stay_copy(self, index):
        return pltpu.make_async_copy(
            self.stay.at[self.region(self.stages[0], index)], self.stay_s, self.stay_sem.at[self.k]
        )

    def stage_copy(self, stage, source):
        return pltpu.make_async_remote_copy(
            src_ref=source,
            dst_ref=self.buffers[stage],
            send_sem=self.send_sem.at[self.k, stage],
            recv_sem=self.recv_sem.at[self.k, stage],
            device_id=self.flips[stage][1],
            device_id_type=MESH,
        )

    def start(self):
        self.core_copy().start()
        self.stay_copy(1 - self.flips[0][0]).start()

    def advance(self):
        if self.at < 0:
            self.at = 0
            mine = self.flips[0][0]
            self.core_copy().wait_recv()
            self.stay_copy(1 - mine).wait()
            away = self.pick(self.core_in, 1 - mine)
            self.core_in[away] = self.core_in[away] + self.stay_s[...]
            self.stay_copy(mine).start()
            self.held = self.core_in
        else:
            mine = self.flips[self.at][0]
            buffer = self.buffers[self.at]
            self.stage_copy(self.at, buffer).wait_recv()
            kept = self.held[self.pick(self.held, mine)]
            if self.at == 0:
                self.stay_copy(mine).wait()
                kept = kept + self.stay_s[...]
            buffer[...] = buffer[...] + kept
            axis, bit = self.stages[self.at]
            if axis == "band":
                self.lead.remove(bit)
            self.held = buffer
            self.at += 1
        if self.at == len(self.stages):
            return True
        self.stage_copy(self.at, self.held.at[self.pick(self.held, 1 - self.flips[self.at][0])]).start()
        return False

    def drain(self):
        self.core_copy().wait_send()
        for stage, buffer in enumerate(self.buffers):
            self.stage_copy(stage, buffer).wait_send()


class FullFlow:
    def __init__(self, held, stages, buffers, send_sem, recv_sem):
        self.held, self.stages, self.buffers = held, stages, buffers
        self.send_sem, self.recv_sem = send_sem, recv_sem
        self.flips = [flip(*stage) for stage in stages]
        self.at = 0

    def copy(self, stage, source):
        return pltpu.make_async_remote_copy(
            src_ref=source,
            dst_ref=self.buffers[stage],
            send_sem=self.send_sem.at[stage],
            recv_sem=self.recv_sem.at[stage],
            device_id=self.flips[stage][1],
            device_id_type=MESH,
        )

    def send(self):
        if self.at < len(self.stages):
            self.copy(self.at, self.held).start()

    def step(self):
        if self.at < len(self.stages):
            buffer = self.buffers[self.at]
            self.copy(self.at, buffer).wait_recv()
            buffer[...] = buffer[...] + self.held[...]
            self.held = buffer
            self.at += 1
            self.send()

    def drain(self):
        for stage, buffer in enumerate(self.buffers):
            self.copy(stage, buffer).wait_send()


def backward_kernel(
    block, members, pairs, grps, plans, slots, vector_stages,
    grad_ref, qkv_ref, key_aux_ref, query_ref, out_full_ref, first_ref,
    weight_ref, start_ref, grad_middle_ref, gain_ref, lead_ref, feed_ref, up_vector_ref, result_ref, *refs,
):
    count = len(plans)
    arrays = max(plan["array"] for plan in plans) + 1
    refs = list(refs)

    def grab(n):
        found = refs[:n]
        del refs[:n]
        return found

    away_refs, stay_refs = grab(arrays), grab(arrays)
    up_ref, down_ref, output_ref, heads_ref, vectors_ref = grab(5)
    own_tokens_ref, other_tokens_ref, other_result_ref, first_other = grab(4)
    grad_in, grad_s, query_s, plain_s, query_sum, out_s, joined_in = grab(7)
    normed_s, heads_s, heads_in, heads_got, heads_sum = grab(5)
    weight_s, joined_s, tokens_s, vectors_s = grab(4)
    core_in, stay_s = grab(count), grab(count)
    buffers = [grab(len(plan["stages"])) for plan in plans]
    vector_buffers = grab(len(vector_stages))
    grp_count = bits(grps)
    heads_buffers = grab(grp_count)
    (
        local_sem, grad_send, grad_recv, out_send, out_recv, query_send, query_recv, first_send, first_recv,
        normed_sem, weight_sem, swap_send, swap_recv, vector_send, vector_recv, far_send, far_recv,
        heads_send, heads_recv, heads_two_send, heads_two_recv, gather_send, gather_recv, own_sem,
    ) = grab(24)
    flow_sems = grab(5)

    rows = key_aux_ref.shape[0]
    width = start_ref.shape[1]
    scale = HEAD_DIM ** (-0.5)
    copies = members // pairs
    band, grp = lax.axis_index("band"), lax.axis_index("grp")
    me = lax.rem(band, members)
    base = band - me
    others = [lax.rem(me + i, members) for i in range(1, members)]
    groups_off = [lax.rem(grp + i, grps) for i in range(1, grps)]
    half, far = flip("band", bits(members))
    core_other = flip("band", 0)[1]
    flows = [
        Flow(k, plan, away_refs[plan["array"]], stay_refs[plan["array"]], core_in[k], stay_s[k], buffers[k], flow_sems)
        for k, plan in enumerate(plans)
    ]
    vectors = FullFlow(vectors_s, vector_stages, vector_buffers, vector_send, vector_recv)
    heads_flow = FullFlow(
        heads_sum, [("grp", b) for b in range(grp_count)], heads_buffers, heads_two_send, heads_two_recv
    )

    barrier = pltpu.get_barrier_semaphore()
    greeted = [(base + other, grp) for other in others] + [(band, g) for g in groups_off] + [far]
    for device in greeted:
        pl.semaphore_signal(barrier, inc=1, device_id=device, device_id_type=MESH)
    pl.semaphore_wait(barrier, len(greeted))

    def remote(source, target, send, recv, device):
        return pltpu.make_async_remote_copy(
            src_ref=source, dst_ref=target, send_sem=send, recv_sem=recv, device_id=device, device_id_type=MESH
        )

    grad_copies = [
        remote(
            grad_ref.at[other // copies], grad_in.at[me], grad_send.at[i], grad_recv.at[i], (base + other, grp)
        )
        for i, other in enumerate(others)
    ]
    for copy in grad_copies:
        copy.start()
    own = pltpu.make_async_copy(grad_ref.at[me // copies], grad_in.at[me], local_sem)
    own.start()
    for flow in flows:
        flow.start()
    first_copy = remote(first_ref, first_other, first_send, first_recv, core_other)
    first_copy.start()
    result_copy = remote(result_ref.at[1 - half], other_result_ref, swap_send.at[0], swap_recv.at[0], far)

    def weight_load(t):
        return pltpu.make_async_copy(
            weight_ref.at[:, pl.ds(t * width, width)], weight_s.at[t % 2], weight_sem.at[t % 2]
        )

    for t in range(2):
        weight_load(t).start()
    query_s[...] = qkv_ref[:, 0].reshape(rows, LANES)
    query_sum[...] = jnp.zeros_like(query_sum)

    gathers = []

    def gather_copies(k):
        plan, flow = plans[k], flows[k]
        target = (up_ref, down_ref, output_ref)[plan["array"]]
        size = plan["columns"][1]
        columns = size >> grp_count
        offset = plan["columns"][0]
        for b in range(grp_count):
            size //= 2
            offset = offset + flip("grp", b)[0] * size
        where = target.at[pl.ds(*plan["rows"]), pl.ds(pl.multiple_of(offset, LANES), columns)]
        held = flow.buffers[-1]
        mine = pltpu.make_async_copy(held, where, own_sem.at[k])
        return [mine] + [
            remote(held, where, gather_send.at[k, i], gather_recv.at[k, i], (band, g))
            for i, g in enumerate(groups_off)
        ]

    def advance(slot):
        for k in slots[slot]:
            if flows[k].advance():
                for copy in gather_copies(k):
                    copy.start()

    advance(0)
    own.wait()
    for copy in grad_copies:
        copy.wait_recv()
    grads = grad_in[...].reshape(rows, LANES)
    plain_s[...] = grads
    wide = grads.astype(F32)
    product = wide * out_full_ref[...]
    for head in range(2):
        inside = in_head(wide.shape, head)
        delta = jnp.sum(jnp.where(inside, product, 0.0), -1, keepdims=True)
        marked = jnp.where(inside, wide, split_terms(-delta, spare_lane(wide.shape, head)))
        grad_s[head] = marked.astype(BF16)

    def sends_to(other):
        return (lax.rem(other, copies) == lax.rem(me, copies)) & (other != me)

    def out_copy(other):
        return remote(
            out_s.at[other, pl.ds(1, 2)],
            joined_in.at[me // copies, pl.ds(1, 2)],
            out_send.at[other // copies],
            out_recv.at[me // copies],
            (base + other, grp),
        )

    def query_copy(other):
        return remote(
            out_s.at[other, 0],
            joined_in.at[me // copies, 0],
            query_send.at[other // copies],
            query_recv.at[me // copies],
            (base + other, grp),
        )

    sub = min(block, 2**19 // rows)

    @pl.loop(0, members)
    def _(i):
        for slot in range(1, 1 + members):
            if slots[slot]:

                @pl.when(i == slot - 1)
                def _(slot=slot):
                    advance(slot)

        other = lax.rem(me + 1 + i, members)
        for low in range(0, block, sub):
            here = pl.ds(pl.multiple_of(other * block + low, sub), sub)
            key = qkv_ref[other, 1, pl.ds(low, sub)]
            value = qkv_ref[other, 2, pl.ds(low, sub)]
            aux = key_aux_ref[here]
            shape = key.shape
            grad_key, grad_value = [], []
            for head in range(2):
                inside = in_head(shape, head)
                spare = spare_lane(shape, head)
                ones = jnp.where((spare >= 2) & (spare <= 4), 1.0, 0.0).astype(BF16)
                probs = jnp.exp(dot_nt(jnp.where(inside, key, aux), query_ref[head]))
                grad_probs = dot_nt(jnp.where(inside, value, ones), grad_s[head])
                grad_scores = (probs * grad_probs).astype(BF16)
                grad_value.append(dot_nn(probs.astype(BF16), plain_s[...]))
                grad_key.append(dot_nn(grad_scores, query_s[...]))
                query_sum[...] += dot_tn(jnp.where(inside, key, jnp.zeros_like(key)), grad_scores)
            first = in_head(shape, 0)
            out_s[other, 1, pl.ds(low, sub)] = (jnp.where(first, grad_key[0], grad_key[1]) * scale).astype(BF16)
            out_s[other, 2, pl.ds(low, sub)] = jnp.where(first, grad_value[0], grad_value[1]).astype(BF16)

        @pl.when(sends_to(other))
        def _():
            out_copy(other).start()

    slot = members + 1
    advance(slot)
    out_s[:, 0] = (query_sum[...].T * scale).astype(BF16).reshape(members, block, LANES)
    for other in others:

        @pl.when(sends_to(other))
        def _():
            query_copy(other).start()

    joined_in[me // copies] = out_s[me]

    advance(slot + 1)
    first_copy.wait()

    def normed_load(i):
        source = (first_ref if i % 2 == 0 else first_other).at[i // 2]
        return pltpu.make_async_copy(source, normed_s.at[i % 2], normed_sem.at[i % 2])

    normed_load(0).start()
    for i in range(members):
        if i + 1 < members:
            normed_load(i + 1).start()
        rows_of = out_s[me ^ i]
        rows_of = jnp.concatenate([rows_of[t] for t in range(3)], -1)
        normed_load(i).wait()
        term = dot_tn(rows_of, normed_s[i % 2])
        heads_s[...] = term if i == 0 else heads_s[...] + term
    whole = heads_s[...].T.astype(BF16).reshape(heads_in.shape)
    heads_in[...] = jnp.where(lax.rem(me, copies) == 0, whole, jnp.zeros_like(whole))
    heads_far = remote(heads_in.at[1 - half], heads_got, far_send, far_recv, far)
    heads_far.start()
    result_copy.start()

    advance(slot + 2)
    for i in range(1, pairs):
        place = lax.rem(me // copies + i, pairs)
        pltpu.make_async_copy(
            joined_in.at[place, pl.ds(1, 2)], joined_in.at[place, pl.ds(1, 2)], out_recv.at[place]
        ).wait()
        pltpu.make_async_copy(joined_in.at[place, 0], joined_in.at[place, 0], query_recv.at[place]).wait()
    grad_first = None
    for t in range(3):
        for pair in range(pairs):
            joined_s[:, pair * LANES : (pair + 1) * LANES] = joined_in[pair, t]
        joined = joined_s[...]
        weight_load(t).wait()
        term = dot_nt(joined, weight_s[t % 2])
        grad_first = term if grad_first is None else grad_first + term
        if t == 0:
            weight_load(2).start()
        if t != 1:
            row = 4 + t // 2
            vectors_s[row : row + 1] = jnp.sum(joined.astype(F32), 0, keepdims=True)
    advance(slot + 3)
    unit, inverse = normalised(start_ref[...])
    at_input, grad_gain, grad_shift = norm_backward(grad_first, gain_ref[...], unit, inverse)
    grad_start = at_input + grad_middle_ref[...]
    run = tokens_s.shape[1]
    split = grad_start.reshape(2, run, width)
    tokens_s[...] = split.astype(BF16)
    tokens_copy = remote(tokens_s.at[1 - half], other_tokens_ref, swap_send.at[1], swap_recv.at[1], far)
    tokens_copy.start()
    own_tokens_ref[...] = jnp.where(half == 0, split[0], split[1])
    vectors_s[0:1] = jnp.sum(lead_ref[...] * grad_start, 0, keepdims=True)
    vectors_s[1:2] = jnp.sum(grad_start, 0, keepdims=True)
    vectors_s[2:3] = grad_gain
    vectors_s[3:4] = grad_shift
    vectors_s[6:10] = feed_ref[0:4]
    for i in range(up_vector_ref.shape[1] // width):
        vectors_s[10 + i : 11 + i] = up_vector_ref[:, i * width : (i + 1) * width]
    for i in range(10 + up_vector_ref.shape[1] // width, vectors_s.shape[0]):
        vectors_s[i : i + 1] = jnp.zeros((1, width), F32)
    vectors.send()

    def heads_copy(i, other):
        return remote(
            heads_got.at[other], heads_sum.at[me // copies], heads_send.at[i], heads_recv.at[me // copies],
            (base + other, grp),
        )

    def heads_begin():
        heads_far.wait_recv()
        heads_got[...] = heads_got[...] + heads_in[half]

        @pl.when(lax.rem(me, copies) == 0)
        def _():
            for i, other in enumerate(others):
                heads_copy(i, other).start()
            heads_sum[me // copies] = heads_got[me]

    def heads_middle():
        for place in range(pairs):

            @pl.when(place * copies != me)
            def _():
                pltpu.make_async_copy(heads_sum.at[place], heads_sum.at[place], heads_recv.at[place]).wait()

        heads_flow.send()

    def heads_end():
        while heads_flow.at < len(heads_flow.stages):
            heads_flow.step()
        for pair in range(pairs):
            for t in range(3):
                column = t * width + pair * LANES
                heads_ref[:, column : column + LANES] = heads_flow.held[pair, :, t * LANES : (t + 1) * LANES]

    extra = [heads_begin, vectors.step, heads_middle, vectors.step, heads_end] + [vectors.step] * len(vector_stages)
    for n, k in enumerate(slots[slot + 4]):
        if flows[k].advance():
            for copy in gather_copies(k):
                copy.start()
        if n % 2 == 1 and extra:
            extra.pop(0)()
    while extra:
        extra.pop(0)()
    vectors_ref[...] = vectors.held[...]

    for copy in grad_copies:
        copy.wait_send()
    for other in others:

        @pl.when(sends_to(other))
        def _():
            out_copy(other).wait_send()
            query_copy(other).wait_send()

    @pl.when(lax.rem(me, copies) == 0)
    def _():
        for i, other in enumerate(others):
            heads_copy(i, other).wait_send()

    for flow in flows + [vectors, heads_flow]:
        flow.drain()
    heads_far.wait_send()
    result_copy.wait()
    tokens_copy.wait()
    for k in range(count):
        for copy in gather_copies(k):
            copy.wait()


def backward(
    grad_blocks, qkv, key_aux, query, out_full, first, weight, start, grad_middle, gain, lead_rows,
    feed_vectors, up_vector, result, away, stay, plans, pairs, bands, grps, collective_id,
):
    members, _, block, _ = qkv.shape
    rows = members * block
    total, width = start.shape
    run = total // 2
    held = width // bands
    inner = up_vector.shape[1]
    arrays, count, grp_count = len(away), len(plans), bits(grps)
    shapes = [Flow.shapes(plan) for plan in plans]
    z_low = bits(bands) - 2
    links = {("band", z_low): "z", ("band", z_low + 1): "Z"}
    link = lambda stage: links.get(stage, "y" if stage[0] == "grp" else "x")
    size = lambda shape: 2 * functools.reduce(lambda m, n: m * n, shape, 1) / 2**20
    longer = rows / 2048
    tasks = [8.0] + [3.4 * longer] * members + [2.0, 4.0 * longer, 5.0, 4.0]
    slots = plan_events(
        [(size(found[0]), [link(stage) for stage in plan["stages"]]) for found, plan in zip(shapes, plans)], tasks
    )
    vector_stages = [("band", b) for b in range(bits(bands))] + [("grp", b) for b in range(grp_count)]
    longest = max(len(plan["stages"]) for plan in plans)
    vmem = pl.BlockSpec(memory_space=pltpu.VMEM)
    anywhere = pl.BlockSpec(memory_space=pl.ANY)
    dma = pltpu.SemaphoreType.DMA
    return pl.pallas_call(
        functools.partial(backward_kernel, block, members, pairs, grps, plans, slots, vector_stages),
        out_shape=(
            jax.ShapeDtypeStruct((held, inner), BF16),
            jax.ShapeDtypeStruct((inner // bands, width), BF16),
            jax.ShapeDtypeStruct((held, width), BF16),
            jax.ShapeDtypeStruct((held, 3 * width), BF16),
            jax.ShapeDtypeStruct((16, width), F32),
            jax.ShapeDtypeStruct((run, width), F32),
            jax.ShapeDtypeStruct((run, width), BF16),
            jax.ShapeDtypeStruct((run, width), BF16),
            jax.ShapeDtypeStruct(first.shape, BF16),
        ),
        in_specs=[anywhere] + [vmem] * 4 + [anywhere] * 2 + [vmem] * 6 + [anywhere] * (1 + 2 * arrays),
        out_specs=(anywhere, anywhere, anywhere, vmem, vmem, vmem, anywhere, anywhere, anywhere),
        scratch_shapes=[
            pltpu.VMEM((members, 1, block, LANES), BF16),
            pltpu.VMEM((2, rows, LANES), BF16),
            pltpu.VMEM((rows, LANES), BF16),
            pltpu.VMEM((rows, LANES), BF16),
            pltpu.VMEM((LANES, rows), F32),
            pltpu.VMEM((members, 3, block, LANES), BF16),
            pltpu.VMEM((pairs, 3, block, LANES), BF16),
            pltpu.VMEM((2, block, width), BF16),
            pltpu.VMEM((3 * LANES, width), F32),
            pltpu.VMEM((2, members, held, 3 * LANES), BF16),
            pltpu.VMEM((members, held, 3 * LANES), BF16),
            pltpu.VMEM((pairs, held, 3 * LANES), BF16),
            pltpu.VMEM((2, width, width), BF16),
            pltpu.VMEM((total, width), BF16),
            pltpu.VMEM((2, run, width), BF16),
            pltpu.VMEM((16, width), F32),
        ]
        + [pltpu.VMEM(found[0], BF16) for found in shapes]
        + [pltpu.VMEM(found[1], BF16) for found in shapes]
        + [pltpu.VMEM(shape, BF16) for found in shapes for shape in found[1:]]
        + [pltpu.VMEM((16, width), F32) for _ in vector_stages]
        + [pltpu.VMEM((pairs, held, 3 * LANES), BF16) for _ in range(grp_count)]
        + [
            dma, dma((members,)), dma((members,)), dma((members,)), dma((members,)), dma((members,)), dma((members,)),
            dma, dma, dma((2,)), dma((2,)), dma((2,)), dma((2,)),
            dma((len(vector_stages),)), dma((len(vector_stages),)), dma, dma,
            dma((members,)), dma((pairs,)), dma((grp_count,)), dma((grp_count,)),
            dma((count, grps)), dma((count, grps)), dma((count,)),
        ]
        + [dma((count,)), dma((count,)), dma((count,)), dma((count, longest)), dma((count, longest))],
        compiler_params=pltpu.CompilerParams(
            vmem_limit_bytes=60 * 2**20, collective_id=collective_id, has_side_effects=True
        ),
        cost_estimate=pl.CostEstimate(
            flops=24 * rows * rows * LANES, bytes_accessed=64 * 2**20, transcendentals=2 * rows * rows
        ),
        name="backward",
    )(
        grad_blocks, qkv, key_aux, query, out_full, first, weight, start, grad_middle, gain.reshape(1, width),
        lead_rows, feed_vectors, up_vector, result.reshape(2, run, width), *away, *stay,
    )


def swap(array, stage):
    axis, bit = stage
    size = lax.axis_size(axis)
    return lax.ppermute(array, axis, [(i, i ^ (1 << bit)) for i in range(size)])


def bit_of(stage):
    axis, bit = stage
    return (lax.axis_index(axis) >> bit) & 1


def take(array, axis, index):
    return lax.dynamic_index_in_dim(array, index, axis, keepdims=False)


def after(value, *others):
    return lax.optimization_barrier((value,) + others)[0]


def bits(size):
    return size.bit_length() - 1


def local(
    tokens,
    lead_index,
    segment,
    valid,
    lead_weight,
    lead_bias,
    first_gain,
    first_shift,
    heads_weight,
    query_bias,
    value_bias,
    output_weight,
    output_bias,
    second_gain,
    second_shift,
    up_weight,
    up_bias,
    down_weight,
    down_bias,
    cotangent,
):
    bands, grps = lax.axis_size("band"), lax.axis_size("grp")
    groups, rows, width = tokens.shape
    total = groups * rows
    pairs = width // LANES
    members = bands // groups
    band = lax.axis_index("band")
    far = ("band", bits(bands) - 1)
    own_group = bit_of(far)
    block = total

    def regroup(array):
        mine, theirs = take(array, 0, own_group), swap(take(array, 0, 1 - own_group), far)
        low = jnp.where(own_group == 0, mine, theirs)
        high = jnp.where(own_group == 0, theirs, mine)
        return jnp.concatenate([low, high], 0)

    def by_member(array):
        return take(array, 0, own_group).reshape(groups, members, rows).transpose(1, 0, 2)

    own_tokens = regroup(tokens)
    seg_rows, valid_rows = by_member(segment), by_member(valid)
    local_seg = take(seg_rows, 0, lax.rem(band, members)).reshape(total, 1)
    lead_days = take(lead_index, 0, own_group).astype(F32) * 0.25
    lead_rows = jnp.where(local_seg == 0, lead_days[0], lead_days[1])
    seg_own, valid_own = seg_rows.reshape(-1), valid_rows.reshape(-1)
    spare = jnp.arange(LANES, dtype=jnp.int32)[None, :] % HEAD_DIM
    query_aux = (spare == seg_own[:, None]).astype(BF16)
    allowed = (spare == seg_own[:, None]) & (valid_own[:, None] == 1)
    key_aux = jnp.where(
        spare < 2, jnp.where(allowed, 0.0, MASKED), jnp.where(spare < 5, 1.0, 0.0)
    ).astype(BF16)
    core = lax.rem(band, 2).astype(jnp.int32).reshape(1)
    head_bias = jnp.stack([query_bias, jnp.zeros_like(query_bias), value_bias]).reshape(3, 1, width)

    late_tokens = after(own_tokens, query_aux, key_aux, head_bias, lead_rows)
    grad_out = regroup(after(cotangent, own_tokens))
    start, first_low, blocks = heads_forward(
        late_tokens, lead_rows, lead_weight, lead_bias, first_gain, first_shift, heads_weight, head_bias
    )
    qkv, attended, out_full, query_marked = attention_forward(blocks, query_aux, key_aux, members, 1)
    attended = after(attended, grad_out)

    def normed_of(offset):
        return lax.ppermute(
            after(first_low, attended), "band", [(i, i ^ offset) for i in range(bands)]
        )

    first_rows = jnp.stack([first_low] + [normed_of(2 * k) for k in range(1, members // 2)])

    (
        result, grad_middle, grad_blocks, down_away, down_stay, up_away, up_stay,
        output_away, output_stay, feed_vectors, grad_up_bias,
    ) = feed(
        core, attended, start, grad_out, output_weight, output_bias, second_gain, second_shift,
        up_weight, up_bias, down_weight, down_bias, bands,
    )
    split = lambda v: v.reshape((2,) * (bits(bands) - 1) + v.shape[1:])
    held_up, held_down, inner = up_stay.shape[1], down_stay.shape[1], up_weight.shape[1]
    lead = [b for b in range(1, bits(bands))][::-1]
    along = {
        "x": [("band", b) for b in range(1, bits(bands) - 2)],
        "y": [("grp", b) for b in range(bits(grps))],
        "z": [("band", bits(bands) - 2)],
        "Z": [("band", bits(bands) - 1)],
    }

    def plan(array, rows_of, columns_of, links):
        stages = [stage for link in links for stage in along[link]]
        return {"array": array, "rows": rows_of, "columns": columns_of, "lead": lead, "stages": stages}

    quarter, fourth = inner // 4, held_down // 4
    up_part = lambda i, links: plan(0, (0, held_up), (i * quarter, quarter), links)
    down_part = lambda i, links: plan(1, (i * fourth, fourth), (0, width), links)
    plans = [
        up_part(0, "yzZx"),
        up_part(1, "xyzZ"),
        up_part(2, "zxyZ"),
        up_part(3, "xyzZ"),
        down_part(0, "xyzZ"),
        down_part(1, "yzZx"),
        down_part(2, "zxyZ"),
        down_part(3, "xyzZ"),
        plan(2, (0, held_up), (0, width), "yzZx"),
    ]
    grad_up, grad_down, grad_output, grad_heads, vectors, own_grads, other_grads, other_result, _ = backward(
        grad_blocks, qkv, key_aux, query_marked, out_full, first_rows, heads_weight, start, grad_middle,
        first_gain, lead_rows, feed_vectors, grad_up_bias, result,
        [split(v) for v in (up_away, down_away, output_away)],
        [split(v) for v in (up_stay, down_stay, output_stay)],
        plans, pairs, bands, grps, 3,
    )
    own_result = take(result.reshape(2, rows, width), 0, own_group)

    def assemble(mine, theirs):
        theirs = theirs.astype(mine.dtype)
        low, high = jnp.where(own_group == 0, mine, theirs), jnp.where(own_group == 0, theirs, mine)
        return jnp.stack([low, high])

    small = take(vectors[:10].reshape(10, bands, width // bands), 1, band)
    grad_up_bias = take(vectors[10 : 10 + up_weight.shape[1] // width].reshape(bands, -1), 0, band)
    wide = lambda v: v.astype(F32)
    return (
        assemble(own_result, other_result),
        assemble(own_grads, other_grads),
        small[0],
        small[1],
        small[2],
        small[3],
        wide(grad_heads),
        small[4],
        small[5],
        wide(grad_output),
        small[6],
        small[7],
        small[8],
        wide(grad_up),
        grad_up_bias,
        wide(grad_down),
        small[9],
    )


def solution(mesh):
    rows = P("grp", "band", None)
    in_specs = (rows, P("grp", None), P("grp", None), P("grp", None)) + (P(),) * 15 + (rows,)
    vector, matrix = P("band"), P("band", None)
    out_specs = (
        rows,
        rows,
        vector,
        vector,
        vector,
        vector,
        matrix,
        vector,
        vector,
        matrix,
        vector,
        vector,
        vector,
        matrix,
        vector,
        matrix,
        vector,
    )
    return jax.shard_map(local, mesh=mesh, in_specs=in_specs, out_specs=out_specs, check_vma=False)
```

time: 1130 us -> 251 us (0.22)
  waiting for transfers between devices: 735 us -> 2.83 us
  Pallas kernels: 0 us -> 213 us
  matrix products: 163 us -> 0 us
  local copies, waits for them, and re-layouts: 76.3 us -> 4.68 us
  blocking collectives: 65.2 us -> 0 us
  other arithmetic: 65.1 us -> 18.3 us
  between operations: 16.1 us -> 1.07 us
    reduce_scatter x4 -> x0, waiting for transfers between devices: 333 us -> none  [the longest x1 108 us: local(): lax.psum_scatter(grad_down.astype(jnp.bfloat16), 'band', scatter_dimensio...]
    while x8 -> x0, waiting for transfers between devices: 242 us -> none
    pallas_call x0 -> x4, Pallas kernels: none -> 213 us  [the longest x1 139 us: backward(): pl.pallas_call(functools.partial(backward_kernel, block, members, pairs,...]
    dot_general x26 -> x0, matrix products: 163 us -> none  [the longest x2 25.4 us: attend_back(): jnp.einsum('rhd,khd->hrk', grad_heads, head_split(value_rows), preferred_...]
    all_gather x2 -> x0, waiting for transfers between devices: 158 us -> none  [the longest x1 79 us: local(): lax.all_gather(local_keys, 'band', axis=1, tiled=True)]
    unnamed x1 -> x0, blocking collectives: 60.3 us -> none
    while x47 -> x0, local copies, waits for them, and re-layouts: 36.5 us -> none
    convert_element_type x18 -> x6, other arithmetic: 43 us -> 8.31 us  [the longest x4 4.9 us: local(): wide = lambda v: v.astype(F32)]
  transfers between devices with their start and end apart: 11 -> 5, of which waited for: 10 -> 1; matrix products, arithmetic and copies ran while one was open for 9% -> 4% of each run, Pallas kernels for 0% -> 30%
where the time goes in v1:
time: 251 us; the launch traced here: 247 us
  Pallas kernels  213 us (85%)
  other arithmetic  18.3 us (7%)
  starting transfers between devices  7.66 us (3%)
  local copies, waits for them, and re-layouts  4.68 us (2%)
  waiting for transfers between devices  2.83 us (1%)
    pallas_call x1, Pallas kernels, backward(): pl.pallas_call(functools.partial(backward_kernel, block, members, pairs,...  139 us
    pallas_call x1, Pallas kernels, attention_forward(): pl.pallas_call(functools.partial(forward_kernel, block, members, pairs),...  40.9 us
    pallas_call x1, Pallas kernels, feed(): pl.pallas_call(feed_kernel, grid_spec=pltpu.PrefetchScalarGridSpec(num_sc...  26.6 us
    pallas_call x1, Pallas kernels, heads_forward(): pl.pallas_call(heads_kernel, grid=(3,), out_shape=(jax.ShapeDtypeStruct((...  6.54 us
  transfers between devices with their start and end apart: 5, of which 1 were waited for; matrix products, arithmetic and copies ran while one was open for 4% of the time, Pallas kernels for 30%

profile of v1, /device:TPU:0, one launch (start us, length us, event | category | flops | bytes accessed | tf_op | source)
XLA Modules:
  0.0 247.0 jit_solution(3399821262162307253)
XLA Ops:
  0.7 0.0 copy-start
  0.7 0.0 copy-start.2
  0.7 0.0 copy-start.3
  0.7 1.1 dynamic-slice_bitcast_fusion.1
  1.8 4.1 %collective-permute-start = (bf16[128,1024]{1,0:T(8,128)(2,1)S(1)}, bf16[128,1024]{1,0:T(8,128)(2,1)S(1)}, u32[]{:S(2)}, u32[]{:S(2)}) collective-permute-start(bf16[128,1024]{1,0:T(8,128)(2,1)S(1)} %dynamic-slice_bitcast_fusion.1), channel_id=1, source_target_pairs={{0,16},{2,18},{4,20},{6,22},{8,24},{10,26},{12,28},{14,30},{16,0},... | collective-permute-start | bytes 786440 | tf_op jit(solution)/shard_map/ppermute | solution.py:1032
  5.9 0.0 copy-done
  5.9 0.7 fusion.6
  6.6 0.6 fusion.17
  7.2 0.8 compare_reduce_fusion
  8.0 0.1 pad.11.clone
  8.1 0.8 pad_maximum_fusion.5
  8.8 0.6 reshape.191.bias_ref
  9.4 1.3 fusion.4
  10.8 0.8 copy.42.lead_ref
  11.6 2.3 select_convert_fusion.key_aux_ref
  13.8 1.1 compare_convert_fusion.query_aux_ref
  15.0 2.8 %collective-permute-done = bf16[128,1024]{1,0:T(8,128)(2,1)S(1)} collective-permute-done((bf16[128,1024]{1,0:T(8,128)(2,1)S(1)}, bf16[128,1024]{1,0:T(8,128)(2,1)S(1)}, u32[]{:S(2)}, u32[]{:S(2)}) %collective-permute-start) | collective-permute-done | bytes 262176 | tf_op jit(solution)/shard_map/ppermute | solution.py:1032
  17.8 0.0 copy-done.2
  17.8 0.8 pad_maximum_fusion.2.tokens_ref
  18.7 0.0 copy-done.3
  18.7 0.1 collective-permute-start.1
  18.8 6.5 %heads_forward.1 = (f32[256,1024]{1,0:T(8,128)}, bf16[256,1024]{1,0:T(8,128)(2,1)}, bf16[8,3,256,128]{3,2,1,0:T(8,128)(2,1)}) custom-call(bf16[256,1024]{1,0:T(8,128)(2,1)} %pad_maximum_fusion.2.tokens_ref, f32[256,1]{1,0:T(8,128)} %copy.42.lead_ref, f32[1,1024]{1,0:T(1,128)} %bitcast.96, f32[1,1024]{1,0:T(1,128)} %bitcast.97, f32[1,1024]{1,0:T(1,128)} %bitcast.99, ...), custom_call_target="tpu_custom_call" | custom-call | flops 1610612736 | bytes 6291456 | tf_op jit(solution)/shard_map/heads_forward/pallas_call | solution.py:270
  25.3 40.9 %attention_forward.1 = (bf16[8,3,256,128]{3,2,1,0:T(8,128)(2,1)}, bf16[8,1,256,128]{3,2,1,0:T(8,128)(2,1)}, f32[2048,128]{1,0:T(8,128)}, bf16[2,2048,128]{2,1,0:T(8,128)(2,1)}) custom-call(bf16[8,3,256,128]{3,2,1,0:T(8,128)(2,1)} %get-tuple-element.48.blocks_ref, bf16[2048,128]{1,0:T(8,128)(2,1)} %compare_convert_fusion.query_aux_ref, ...), custom_call_target="tpu_custom_call" | custom-call | flops 4294967296 | bytes 33554432 | tf_op jit(solution)/shard_map/attention_forward/pallas_call | solution.py:183
  66.2 0.0 copy-start.6
  66.2 0.0 collective-permute-done.1
  66.3 0.8 pad_maximum_fusion.3.grad_ref
  67.1 0.2 copy-done.6
  67.3 0.0 collective-permute-start.2
  67.3 0.7 collective-permute-start.3
  68.0 2.8 %collective-permute-start.4 = (bf16[256,1024]{1,0:T(8,128)(2,1)S(1)}, bf16[256,1024]{1,0:T(8,128)(2,1)S(1)}, u32[]{:S(2)}, u32[]{:S(2)}) collective-permute-start(bf16[256,1024]{1,0:T(8,128)(2,1)S(1)} %copy-done.6), channel_id=1, source_target_pairs={{0,12},{2,14},{4,8},{6,10},{8,4},{10,6},{12,0},{14,2},{16,28},{18,... | collective-permute-start | bytes 1572872 | tf_op jit(solution)/shard_map/ppermute | solution.py:1117
  70.8 26.6 %feed.1 = (bf16[256,1024]{1,0:T(8,128)(2,1)}, f32[256,1024]{1,0:T(8,128)}, bf16[8,1,256,128]{3,2,1,0:T(8,128)(2,1)}, bf16[8,256,1024]{2,1,0:T(8,128)(2,1)}, bf16...) custom-call(s32[1]{0:T(128)} %bitcast.core_ref, ...), custom_call_target="tpu_custom_call" | custom-call | flops 12884901888 | bytes 33554432 | tf_op jit(solution)/shard_map/feed/pallas_call | solution.py:368
  97.4 0.0 collective-permute-done.2
  97.4 0.0 collective-permute-done.3
  97.4 0.0 collective-permute-done.4
  97.4 1.6 pad_maximum_fusion.first_ref
  99.0 0.0 copy-start.9
  99.0 138.5 %backward.1 = (bf16[64,4096]{1,0:T(8,128)(2,1)}, bf16[256,1024]{1,0:T(8,128)(2,1)}, bf16[64,1024]{1,0:T(8,128)(2,1)}, bf16[64,3072]{1,0:T(8,128)(2,1)}, f32[16,1...) custom-call(bf16[8,1,256,128]{3,2,1,0:T(8,128)(2,1)} %get-tuple-elem, ...), custom_call_target="tpu_custom_call" | custom-call | flops 12884901888 | bytes 67108864 | tf_op jit(solution)/shard_map/backward/pallas_call | solution.py:970
  237.5 0.0 copy-start.4
  237.5 0.0 copy-done.9
  237.6 0.0 copy-start.7
  237.6 1.1 fusion.2
  238.6 0.0 copy-start.10
  238.6 0.0 copy-start.11
  238.7 0.0 copy-start.5
  238.7 0.0 copy-start.8
  238.7 2.2 convert_element_type.31
  240.8 0.0 copy-done.4
  240.8 1.1 convert_element_type.32
  241.9 0.0 copy-done.7
  241.9 0.9 convert_element_type.29
  242.9 0.0 copy-done.10
  242.9 0.7 convert_element_type.30
  243.6 0.0 copy-done.11
  243.6 0.1 reshape.208
  243.7 0.0 copy-start.1
  243.7 0.0 copy-done.5
  243.7 0.0 copy-done.8
  243.7 0.1 fusion
  243.8 1.1 pad_maximum_fusion.1
  244.9 0.8 pad_maximum_fusion.4
  245.8 0.6 constant_dynamic-slice_fusion.9
  246.3 0.6 fusion.7
  246.9 0.0 copy-done.1
  (12 shorter events, 0.2 us)
Async XLA Ops:
  0.7 5.2 %copy-start = (s32[2,2048]{1,0:T(2,128)S(1)}, s32[2,2048]{1,0:T(2,128)}, u32[]{:S(2)}) copy-start(s32[2,2048]{1,0:T(2,128)} %param.22) | copy-start | bytes 49156
  0.7 17.1 %copy-start.2 = (bf16[2,128,1024]{2,1,0:T(8,128)(2,1)S(1)}, bf16[2,128,1024]{2,1,0:T(8,128)(2,1)}, u32[]{:S(2)}) copy-start(bf16[2,128,1024]{2,1,0:T(8,128)(2,1)} %param.20) | copy-start | bytes 1572868
  0.7 18.0 %copy-start.3 = (bf16[2,128,1024]{2,1,0:T(8,128)(2,1)S(1)}, bf16[2,128,1024]{2,1,0:T(8,128)(2,1)}, u32[]{:S(2)}) copy-start(bf16[2,128,1024]{2,1,0:T(8,128)(2,1)} %param.39) | copy-start | bytes 1572868
  1.8 16.0 %collective-permute-start = (bf16[128,1024]{1,0:T(8,128)(2,1)S(1)}, bf16[128,1024]{1,0:T(8,128)(2,1)S(1)}, u32[]{:S(2)}, u32[]{:S(2)}) collective-permute-start(bf16[128,1024]{1,0:T(8,128)(2,1)S(1)} %dynamic-slice_bitcast_fusion.1), channel_id=1, source_target_pairs={{0,16},{2,18},{4,20},{6,22},{8,24},{10,26},{12,28},{14,30},{16,0},... | collective-permute-start | bytes 786440 | tf_op jit(solution)/shard_map/ppermute | solution.py:1032
  18.7 47.5 %collective-permute-start.1 = (bf16[128,1024]{1,0:T(8,128)(2,1)S(1)}, bf16[128,1024]{1,0:T(8,128)(2,1)S(1)}, u32[]{:S(2)}, u32[]{:S(2)}) collective-permute-start(bf16[128,1024]{1,0:T(8,128)(2,1)S(1)} %dynamic-slice_bitcast_fusion), channel_id=1, source_target_pairs={{0,16},{2,18},{4,20},{6,22},{8,24},{10,26},{12,28},{14,30},{16,0},... | collective-permute-start | bytes 786440 | tf_op jit(solution)/shard_map/ppermute | solution.py:1032
  66.2 1.1 copy-start.6
  67.3 30.1 %collective-permute-start.2 = (bf16[256,1024]{1,0:T(8,128)(2,1)S(1)}, bf16[256,1024]{1,0:T(8,128)(2,1)S(1)}, u32[]{:S(2)}, u32[]{:S(2)}) collective-permute-start(bf16[256,1024]{1,0:T(8,128)(2,1)S(1)} %copy-done.6), channel_id=1, source_target_pairs={{0,4},{2,6},{4,0},{6,2},{8,12},{10,14},{12,8},{14,10},{16,20},{18,... | collective-permute-start | bytes 1572872 | tf_op jit(solution)/shard_map/ppermute | solution.py:1117
  67.3 30.1 %collective-permute-start.3 = (bf16[256,1024]{1,0:T(8,128)(2,1)S(1)}, bf16[256,1024]{1,0:T(8,128)(2,1)S(1)}, u32[]{:S(2)}, u32[]{:S(2)}) collective-permute-start(bf16[256,1024]{1,0:T(8,128)(2,1)S(1)} %copy-done.6), channel_id=1, source_target_pairs={{0,8},{2,10},{4,12},{6,14},{8,0},{10,2},{12,4},{14,6},{16,24},{18,... | collective-permute-start | bytes 1572872 | tf_op jit(solution)/shard_map/ppermute | solution.py:1117
  68.0 29.4 %collective-permute-start.4 = (bf16[256,1024]{1,0:T(8,128)(2,1)S(1)}, bf16[256,1024]{1,0:T(8,128)(2,1)S(1)}, u32[]{:S(2)}, u32[]{:S(2)}) collective-permute-start(bf16[256,1024]{1,0:T(8,128)(2,1)S(1)} %copy-done.6), channel_id=1, source_target_pairs={{0,12},{2,14},{4,8},{6,10},{8,4},{10,6},{12,0},{14,2},{16,28},{18,... | collective-permute-start | bytes 1572872 | tf_op jit(solution)/shard_map/ppermute | solution.py:1117
  99.0 138.5 %copy-start.9 = (bf16[256,1024]{1,0:T(8,128)(2,1)S(1)}, bf16[256,1024]{1,0:T(8,128)(2,1)}, u32[]{:S(2)}) copy-start(bf16[256,1024]{1,0:T(8,128)(2,1)} %get-tuple-element.53) | copy-start | bytes 1572868
  237.5 3.3 %copy-start.4 = (bf16[256,1024]{1,0:T(8,128)(2,1)S(1)}, bf16[256,1024]{1,0:T(8,128)(2,1)}, u32[]{:S(2)}) copy-start(bf16[256,1024]{1,0:T(8,128)(2,1)} %get-tuple-element.76) | copy-start | bytes 1572868
  237.6 4.4 %copy-start.7 = (bf16[64,3072]{1,0:T(8,128)(2,1)S(1)}, bf16[64,3072]{1,0:T(8,128)(2,1)}, u32[]{:S(2)}) copy-start(bf16[64,3072]{1,0:T(8,128)(2,1)} %get-tuple-element.73) | copy-start | bytes 1179652
  238.6 4.2 %copy-start.10 = (bf16[64,1024]{1,0:T(8,128)(2,1)S(1)}, bf16[64,1024]{1,0:T(8,128)(2,1)}, u32[]{:S(2)}) copy-start(bf16[64,1024]{1,0:T(8,128)(2,1)} %get-tuple-element.74) | copy-start | bytes 393220
  238.6 4.9 %copy-start.11 = (f32[16,1024]{1,0:T(8,128)S(1)}, f32[16,1024]{1,0:T(8,128)}, u32[]{:S(2)}) copy-start(f32[16,1024]{1,0:T(8,128)} %get-tuple-element.72) | copy-start | bytes 196612
  238.7 5.0 %copy-start.5 = (f32[128,1024]{1,0:T(8,128)S(1)}, f32[128,1024]{1,0:T(8,128)}, u32[]{:S(2)}) copy-start(f32[128,1024]{1,0:T(8,128)} %get-tuple-element.70) | copy-start | bytes 1572868
  238.7 5.0 %copy-start.8 = (bf16[128,1024]{1,0:T(8,128)(2,1)S(1)}, bf16[128,1024]{1,0:T(8,128)(2,1)}, u32[]{:S(2)}) copy-start(bf16[128,1024]{1,0:T(8,128)(2,1)} %get-tuple-element.71) | copy-start | bytes 786436
  243.7 3.2 %copy-start.1 = (s32[2,2048]{1,0:T(2,128)S(1)}, s32[2,2048]{1,0:T(2,128)}, u32[]{:S(2)}) copy-start(s32[2,2048]{1,0:T(2,128)} %param.22) | copy-start | bytes 49156

commit v2 on v1

--- a/solution.py
+++ b/solution.py
@@ -65,50 +65,122 @@
 
 def forward_kernel(
     block, members, pairs,
-    blocks_ref, query_aux_ref, key_aux_ref,
-    qkv_ref, attended_ref, out_full_ref, query_ref,
-    qkv_in, key_s, value_s, out_s,
-    local_sem, keep_sem, qkv_send, qkv_recv, out_send, out_recv,
+    tokens_ref, cotangent_ref, lead_ref, segment_ref, valid_ref, lead_weight_ref, lead_bias_ref, gain_ref, shift_ref,
+    weight_ref, query_bias_ref, value_bias_ref,
+    qkv_ref, attended_ref, grads_ref, start_ref, first_ref, lead_out_ref, key_aux_ref, out_full_ref, query_ref,
+    tokens_s, weight_s, blocks_s, query_aux, segment_s, qkv_in, key_s, value_s, out_s,
+    token_sem, swap_send, swap_recv, weight_sem, local_sem, keep_sem, qkv_send, qkv_recv, out_send, out_recv,
 ):
     rows = members * block
+    run = block // 2
+    width = start_ref.shape[1]
     scale = HEAD_DIM ** (-0.5)
     copies = members // pairs
     band, grp = lax.axis_index("band"), lax.axis_index("grp")
     me = lax.rem(band, members)
     base = band - me
     others = [lax.rem(me + i, members) for i in range(1, members)]
+    half, far = flip("band", bits(members))
 
     barrier = pltpu.get_barrier_semaphore()
-    for other in others:
-        pl.semaphore_signal(barrier, inc=1, device_id=(base + other, grp), device_id_type=MESH)
-    pl.semaphore_wait(barrier, len(others))
+    greeted = [(base + other, grp) for other in others] + [far]
+    for device in greeted:
+        pl.semaphore_signal(barrier, inc=1, device_id=device, device_id_type=MESH)
+    pl.semaphore_wait(barrier, len(greeted))
 
     def remote(source, target, send, recv, device):
         return pltpu.make_async_remote_copy(
             src_ref=source, dst_ref=target, send_sem=send, recv_sem=recv, device_id=device, device_id_type=MESH
         )
 
-    qkv_copies = {}
+    tokens_swap = remote(tokens_ref.at[1 - half], tokens_s.at[1], swap_send.at[0], swap_recv.at[0], far)
+    tokens_swap.start()
+    own_tokens = pltpu.make_async_copy(tokens_ref.at[half], tokens_s.at[0], token_sem)
+    own_tokens.start()
+    own_run = pl.ds(pl.multiple_of(half * run, run), run)
+    other_run = pl.ds(pl.multiple_of((1 - half) * run, run), run)
+
+    def weight_load(t):
+        return pltpu.make_async_copy(weight_ref.at[:, pl.ds(t * width, width)], weight_s.at[t], weight_sem.at[t])
+
     for t in (1, 2, 0):
-        for i, other in enumerate(others):
-            qkv_copies[t, i] = remote(
-                blocks_ref.at[other // copies, t],
-                qkv_in.at[me, t],
-                qkv_send.at[t, i],
-                qkv_recv.at[t, i],
-                (base + other, grp),
-            )
-            qkv_copies[t, i].start()
-    own = pltpu.make_async_copy(blocks_ref.at[me // copies], qkv_in.at[me], local_sem)
-    own.start()
-    own.wait()
-    for i in range(members - 1):
-        qkv_copies[1, i].wait_recv()
+        weight_load(t).start()
+
+    def in_order(ref):
+        value = jnp.where(half == 0, ref[0:1], ref[1:2])
+        pieces = [
+            value[:, (j + r * members) * run : (j + r * members + 1) * run] for j in range(members) for r in range(2)
+        ]
+        return jnp.concatenate(pieces, -1)
+
+    segment, valid = in_order(segment_ref), in_order(valid_ref)
+    segment_s[...] = segment
+    place = lax.broadcasted_iota(jnp.int32, (8, rows), 0)
+    hidden = lambda sample: jnp.where((segment == sample) & (valid == 1), 0.0, MASKED)
+    feature = jnp.where(place == 0, hidden(0), jnp.where(place == 1, hidden(1), 0.0))
+    feature = jnp.where(place == 2, 1.0, feature)
+    feature = jnp.where(place == 3, (segment == 0).astype(F32), feature)
+    feature = jnp.where(place == 4, (segment == 1).astype(F32), feature).astype(BF16)
+    row = lax.broadcasted_iota(jnp.int32, (8, LANES), 0)
+    spare = lax.broadcasted_iota(jnp.int32, (8, LANES), 1) % HEAD_DIM
+    for_key = ((row < 2) & (spare == row)) | ((row == 2) & (spare >= 2) & (spare <= 4))
+    for_query = (row >= 3) & (row <= 4) & (spare == row - 3)
+    key_aux_ref[...] = dot_tn(feature, for_key.astype(BF16)).astype(BF16)
+    query_aux[...] = dot_tn(feature, for_query.astype(BF16)).astype(BF16)
+    days = lead_ref[...].astype(F32) * 0.25
+    days = jnp.where(half == 0, days[0:1], days[1:2])
+    own_segment = segment_s[:, pl.ds(pl.multiple_of(me * block, block), block)]
+    lead = jnp.where(own_segment == 0, days[:, 0:1], days[:, 1:2])
+    lead = jnp.where(lax.broadcasted_iota(jnp.int32, (8, block), 0) == 0, lead, 0.0).astype(BF16)
+    lead_out_ref[...] = dot_tn(lead, (row == 0).astype(BF16))
+
+    def qkv_copy(t, phase, i, other):
+        here = own_run if phase == 0 else other_run
+        return remote(
+            blocks_s.at[other // copies, t, here],
+            qkv_in.at[me, t, here],
+            qkv_send.at[t, phase, i],
+            qkv_recv.at[t, phase, i],
+            (base + other, grp),
+        )
+
+    def project(phase):
+        here = own_run if phase == 0 else other_run
+        lead_here = jnp.concatenate([lead_out_ref[here]] * (width // LANES), -1)
+        start = tokens_s[phase].astype(F32) + lead_here * lead_weight_ref[...] + lead_bias_ref[...]
+        start_ref[here] = start
+        first = (normalised(start)[0] * gain_ref[...] + shift_ref[...]).astype(BF16)
+        first_ref[here] = first
+        for t in (1, 2, 0):
+            if phase == 0:
+                weight_load(t).wait()
+            joined = dot_nn(first, weight_s[t])
+            if t != 1:
+                joined = joined + (query_bias_ref if t == 0 else value_bias_ref)[...]
+            joined = joined.astype(BF16)
+            for pair in range(pairs):
+                blocks_s[pair, t, here] = joined[:, pair * LANES : (pair + 1) * LANES]
+            for i, other in enumerate(others):
+                qkv_copy(t, phase, i, other).start()
+            qkv_in[me, t, here] = blocks_s[me // copies, t, here]
+
+    own_tokens.wait()
+    project(0)
+    tokens_swap.wait_recv()
+    grads_swap = remote(cotangent_ref.at[1 - half], grads_ref.at[own_run], swap_send.at[1], swap_recv.at[1], far)
+    grads_own = pltpu.make_async_copy(cotangent_ref.at[half], grads_ref.at[own_run], local_sem)
+    project(1)
+    grads_own.start()
+
+    for i, other in enumerate(others):
+        for phase in range(2):
+            qkv_copy(1, phase, i, other).wait_recv()
     keys = qkv_in[:, 1].reshape(rows, LANES)
     for head in range(2):
         key_s[head] = jnp.where(in_head(keys.shape, head), keys, key_aux_ref[...])
-    for i in range(members - 1):
-        qkv_copies[2, i].wait_recv()
+    for i, other in enumerate(others):
+        for phase in range(2):
+            qkv_copy(2, phase, i, other).wait_recv()
     value_s[...] = qkv_in[:, 2].reshape(rows, LANES)
 
     def sends_to(other):
@@ -129,11 +201,13 @@
 
         @pl.when(i > 0)
         def _():
-            pltpu.make_async_copy(qkv_in.at[other, 0], qkv_in.at[other, 0], qkv_recv.at[0, i - 1]).wait()
+            for phase, here in enumerate((own_run, other_run)):
+                landed = qkv_in.at[other, 0, here]
+                pltpu.make_async_copy(landed, landed, qkv_recv.at[0, phase, i - 1]).wait()
 
         here = pl.ds(pl.multiple_of(other * block, block), block)
         query = qkv_in[other, 0].astype(F32) * scale
-        aux = query_aux_ref[here].astype(F32)
+        aux = query_aux[here].astype(F32)
         shape = query.shape
         mixed = []
         for head in range(2):
@@ -155,14 +229,22 @@
         def _():
             out_copy(other).start()
 
+        @pl.when(i == 0)
+        def _():
+            grads_swap.start()
+
     keep = pltpu.make_async_copy(qkv_in, qkv_ref, keep_sem)
     keep.start()
-    own_out = pltpu.make_async_copy(out_s.at[me], attended_ref.at[me // copies], local_sem)
+    own_out = pltpu.make_async_copy(out_s.at[me], attended_ref.at[me // copies], token_sem)
     own_out.start()
     keep.wait()
     own_out.wait()
-    for copy in qkv_copies.values():
-        copy.wait_send()
+    grads_own.wait()
+    tokens_swap.wait_send()
+    for t in range(3):
+        for phase in range(2):
+            for i, other in enumerate(others):
+                qkv_copy(t, phase, i, other).wait_send()
     for other in others:
 
         @pl.when(sends_to(other))
@@ -172,11 +254,19 @@
     for i in range(1, pairs):
         slot = lax.rem(me // copies + i, pairs)
         pltpu.make_async_copy(attended_ref.at[slot], attended_ref.at[slot], out_recv.at[slot]).wait()
-
-
-def attention_forward(blocks, query_aux, key_aux, members, collective_id):
-    pairs, _, block, _ = blocks.shape
+    grads_swap.wait_send()
+    pltpu.make_async_copy(grads_ref.at[other_run], grads_ref.at[other_run], swap_recv.at[1]).wait()
+
+
+def forward(
+    tokens, cotangent, lead_index, segment, valid, lead_weight, lead_bias, gain, shift, weight, query_bias,
+    value_bias, members, collective_id,
+):
+    _, run, width = tokens.shape
+    block = 2 * run
     rows = members * block
+    pairs = width // LANES
+    row = lambda v: v.reshape(1, width)
     vmem = pl.BlockSpec(memory_space=pltpu.VMEM)
     anywhere = pl.BlockSpec(memory_space=pl.ANY)
     dma = pltpu.SemaphoreType.DMA
@@ -185,17 +275,28 @@
         out_shape=(
             jax.ShapeDtypeStruct((members, 3, block, LANES), BF16),
             jax.ShapeDtypeStruct((pairs, 1, block, LANES), BF16),
+            jax.ShapeDtypeStruct((block, width), BF16),
+            jax.ShapeDtypeStruct((block, width), F32),
+            jax.ShapeDtypeStruct((block, width), BF16),
+            jax.ShapeDtypeStruct((block, LANES), F32),
+            jax.ShapeDtypeStruct((rows, LANES), BF16),
             jax.ShapeDtypeStruct((rows, LANES), F32),
             jax.ShapeDtypeStruct((2, rows, LANES), BF16),
         ),
-        in_specs=[anywhere, vmem, vmem],
-        out_specs=(anywhere, anywhere, vmem, vmem),
+        in_specs=[anywhere, anywhere] + [vmem] * 7 + [anywhere, vmem, vmem],
+        out_specs=(anywhere, anywhere, anywhere) + (vmem,) * 6,
         scratch_shapes=[
+            pltpu.VMEM((2, run, width), BF16),
+            pltpu.VMEM((3, width, width), BF16),
+            pltpu.VMEM((pairs, 3, block, LANES), BF16),
+            pltpu.VMEM((rows, LANES), BF16),
+            pltpu.VMEM((1, rows), jnp.int32),
             pltpu.VMEM((members, 3, block, LANES), BF16),
             pltpu.VMEM((2, rows, LANES), BF16),
             pltpu.VMEM((rows, LANES), BF16),
             pltpu.VMEM((members, 1, block, LANES), BF16),
-            dma, dma, dma((3, members)), dma((3, members)), dma((members,)), dma((members,)),
+            dma, dma((2,)), dma((2,)), dma((3,)), dma, dma,
+            dma((3, 2, members)), dma((3, 2, members)), dma((members,)), dma((members,)),
         ],
         compiler_params=pltpu.CompilerParams(
             vmem_limit_bytes=VMEM_BYTES, collective_id=collective_id, has_side_effects=True
@@ -203,8 +304,11 @@
         cost_estimate=pl.CostEstimate(
             flops=8 * rows * rows * LANES, bytes_accessed=32 * 2**20, transcendentals=2 * rows * rows
         ),
-        name="attention_forward",
-    )(blocks, query_aux, key_aux)
+        name="forward",
+    )(
+        tokens, cotangent, lead_index, segment, valid, row(lead_weight), row(lead_bias), row(gain), row(shift),
+        weight, row(query_bias), row(value_bias),
+    )
 
 
 def device_at(axis, index):
@@ -242,56 +346,8 @@
     stay_ref[...] = jnp.where(core == 0, even, odd)
 
 
-def heads_kernel(
-    tokens_ref, lead_ref, lead_weight_ref, lead_bias_ref, gain_ref, shift_ref, weight_ref, bias_ref,
-    start_ref, first_ref, out_ref,
-):
-    part = pl.program_id(0)
-
-    @pl.when(part == 0)
-    def _():
-        start = tokens_ref[...].astype(F32) + lead_ref[...] * lead_weight_ref[...] + lead_bias_ref[...]
-        start_ref[...] = start
-        first_ref[...] = (normalised(start)[0] * gain_ref[...] + shift_ref[...]).astype(BF16)
-
-    joined = (dot_nn(first_ref[...], weight_ref[...]) + bias_ref[0]).astype(BF16)
-    for pair in range(out_ref.shape[0]):
-        out_ref[pair, 0] = joined[:, pair * LANES : (pair + 1) * LANES]
-
-
 def constant(*shape):
     return pl.BlockSpec(shape, lambda *i: (0,) * len(shape))
-
-
-def heads_forward(tokens, lead_rows, lead_weight, lead_bias, gain, shift, weight, bias):
-    total, width = tokens.shape
-    pairs = width // LANES
-    row = lambda v: v.reshape(1, width)
-    return pl.pallas_call(
-        heads_kernel,
-        grid=(3,),
-        out_shape=(
-            jax.ShapeDtypeStruct((total, width), F32),
-            jax.ShapeDtypeStruct((total, width), BF16),
-            jax.ShapeDtypeStruct((pairs, 3, total, LANES), BF16),
-        ),
-        in_specs=[constant(total, width), constant(total, 1)]
-        + [constant(1, width)] * 4
-        + [
-            pl.BlockSpec((width, width), lambda i: (0, i)),
-            pl.BlockSpec((1, 1, width), lambda i: (i, 0, 0)),
-        ],
-        out_specs=(
-            constant(total, width),
-            constant(total, width),
-            pl.BlockSpec((pairs, 1, total, LANES), lambda i: (0, i, 0, 0)),
-        ),
-        compiler_params=pltpu.CompilerParams(vmem_limit_bytes=VMEM_BYTES),
-        cost_estimate=pl.CostEstimate(
-            flops=6 * total * width * width, bytes_accessed=6 * width * width, transcendentals=0
-        ),
-        name="heads_forward",
-    )(tokens, lead_rows, row(lead_weight), row(lead_bias), row(gain), row(shift), weight, bias)
 
 
 def feed_kernel(
@@ -359,7 +415,7 @@
     total, width = start.shape
     inner = up.shape[1]
     pairs = width // LANES
-    chunk = 512
+    chunk = 1024
     held, held_down = width // bands, inner // bands
     per_chunk = chunk // held_down // 2
     row = lambda v: v.reshape(1, -1)
@@ -431,42 +487,127 @@
     )
 
 
-LINK = 22.3
-CORE = 1.5
-ADD = 0.35
-HOP = 1.5
-
-
-def plan_events(parts, tasks):
-    free, waiting, slots, now = {}, [], [[] for _ in range(len(tasks) + 1)], 0.0
-    ready = 3.0
-    for k, (size, links) in enumerate(parts):
-        ready += size * CORE
-        waiting.append((ready, k, size, list(links)))
-    for slot in range(len(tasks) + 1):
-        while waiting:
-            waiting.sort()
-            if slot < len(tasks) and waiting[0][0] > now:
+LINK = 26.0
+CORE = 1.55
+ADD = 0.4
+HOP = 4.0
+
+
+def plan_steps(sizes, stages, vector_stages, iterations, iteration, slack, late_slack):
+    free = {link: 0.0 for link in ("x", "y", "z", "Z", "core")}
+    held, left, orders = list(sizes), [list(stages) for _ in sizes], [[] for _ in sizes]
+    ready, waiting, steps, count = [], [], [], 0
+    now = 3.0
+
+    def occupy(link, size):
+        if link == "Z":
+            free["Z"] = max(now, free["Z"]) + 2 * size * LINK
+            free["z"] = max(now, free["z"]) + size * LINK
+        else:
+            free[link] = max(now, free[link]) + size * (CORE if link == "core" else LINK)
+        return free[link] + HOP
+
+    def expect(arrival, name, argument=None):
+        nonlocal count
+        count += 1
+        waiting.append((arrival, count, name, argument))
+
+    def send_ready(limit):
+        sent = True
+        while sent:
+            sent = False
+            for link in sorted("xyzZ", key=lambda l: free[l]):
+                fit = [
+                    k
+                    for k in ready
+                    if any(stages[s] == link for s in left[k])
+                    and (link != "Z" or len(orders[k]) >= len(stages) - 1)
+                ]
+                if free[link] - now >= limit or not fit:
+                    continue
+                k = max(fit, key=lambda k: len(left[k]))
+                stage = [s for s in left[k] if stages[s] == link][0]
+                left[k].remove(stage)
+                orders[k].append(stage)
+                held[k] /= 2
+                ready.remove(k)
+                steps.append(("send", k))
+                expect(occupy(link, held[k]), "take", k)
+                sent = True
                 break
-            arrival, k, size, links = waiting.pop(0)
-            now = max(now, arrival) + size * ADD
-            slots[slot].append(k)
-            if links:
-                link = links.pop(0)
-                size /= 2
-                begin = max(now, free.get(link, 0.0))
-                if link == "Z":
-                    end = begin + 2 * size * LINK
-                    free["z"] = max(free.get("z", 0.0), now) + size * LINK
-                else:
-                    end = begin + size * LINK
-                free[link] = end
-                waiting.append((end + HOP, k, size, links))
+
+    def vector_hop(name, hop):
+        if hop < len(vector_stages):
+            expect(occupy(stages.get(vector_stages[hop], "core"), 0.035), name, hop)
+
+    def perform(name, argument):
+        nonlocal now
+        steps.append((name, argument))
+        if name == "take":
+            k = argument
+            now += held[k] * ADD + 0.1
+            if left[k]:
+                ready.append(k)
             else:
-                free["y"] = max(now, free.get("y", 0.0)) + size * LINK
-        if slot < len(tasks):
-            now += tasks[slot]
-    return slots
+                occupy("y", held[k])
+        elif name in ("early", "late"):
+            now += 0.2
+            vector_hop(name, argument + 1)
+        elif name == "grads":
+            now += 3.0
+            expect(now, "iteration", 0)
+        elif name == "iteration":
+            now += iteration
+            for link in "xz":
+                occupy(link, 0.5 / iterations)
+            if argument + 1 < iterations:
+                expect(now, "iteration", argument + 1)
+            else:
+                expect(now, "queries")
+        elif name == "queries":
+            now += 2.0
+            expect(max(occupy("x", 0.25), occupy("z", 0.25)), "joined")
+            expect(now, "products")
+        elif name == "products":
+            now += 4.5
+            expect(occupy("y", 0.19), "near")
+        elif name == "joined":
+            now += 5.0
+            expect(now, "start")
+        elif name == "start":
+            now += 3.0
+            occupy("Z", 0.25)
+            vector_hop("late", 0)
+        elif name == "near":
+            now += 0.3
+            expect(occupy("Z", 0.1), "far")
+        elif name == "far":
+            now += 0.3
+            expect(max(occupy("x", 0.06), occupy("z", 0.06)), "members")
+        elif name == "members":
+            now += 0.3
+            expect(occupy("y", 0.1), "rows")
+        elif name == "rows":
+            now += 0.5
+
+    expect(max(occupy("x", 0.25), occupy("z", 0.25)), "grads")
+    for k, size in enumerate(sizes):
+        expect(occupy("core", size), "take", k)
+    occupy("Z", 0.25)
+    vector_hop("early", 0)
+    main = ("grads", "iteration", "queries", "products", "joined", "start")
+    while waiting or ready:
+        if not waiting:
+            send_ready(1e9)
+        arrived = [w for w in waiting if w[0] <= now]
+        others = [w for w in arrived if w[2] not in main]
+        chosen = min(others or arrived or waiting)
+        waiting.remove(chosen)
+        now = max(now, chosen[0])
+        perform(*chosen[2:])
+        looped = any(w[2] in ("grads", "iteration") for w in waiting)
+        send_ready(slack if looped else late_slack)
+    return orders, steps, now, free
 
 
 class Flow:
@@ -543,7 +684,7 @@
         self.core_copy().start()
         self.stay_copy(1 - self.flips[0][0]).start()
 
-    def advance(self):
+    def take(self):
         if self.at < 0:
             self.at = 0
             mine = self.flips[0][0]
@@ -553,24 +694,24 @@
             self.core_in[away] = self.core_in[away] + self.stay_s[...]
             self.stay_copy(mine).start()
             self.held = self.core_in
-        else:
-            mine = self.flips[self.at][0]
-            buffer = self.buffers[self.at]
-            self.stage_copy(self.at, buffer).wait_recv()
-            kept = self.held[self.pick(self.held, mine)]
-            if self.at == 0:
-                self.stay_copy(mine).wait()
-                kept = kept + self.stay_s[...]
-            buffer[...] = buffer[...] + kept
-            axis, bit = self.stages[self.at]
-            if axis == "band":
-                self.lead.remove(bit)
-            self.held = buffer
-            self.at += 1
-        if self.at == len(self.stages):
-            return True
+            return False
+        mine = self.flips[self.at][0]
+        buffer = self.buffers[self.at]
+        self.stage_copy(self.at, buffer).wait_recv()
+        kept = self.held[self.pick(self.held, mine)]
+        if self.at == 0:
+            self.stay_copy(mine).wait()
+            kept = kept + self.stay_s[...]
+        buffer[...] = buffer[...] + kept
+        axis, bit = self.stages[self.at]
+        if axis == "band":
+            self.lead.remove(bit)
+        self.held = buffer
+        self.at += 1
+        return self.at == len(self.stages)
+
+    def send(self):
         self.stage_copy(self.at, self.held.at[self.pick(self.held, 1 - self.flips[self.at][0])]).start()
-        return False
 
     def drain(self):
         self.core_copy().wait_send()
@@ -614,35 +755,36 @@
 
 
 def backward_kernel(
-    block, members, pairs, grps, plans, slots, vector_stages,
-    grad_ref, qkv_ref, key_aux_ref, query_ref, out_full_ref, first_ref,
-    weight_ref, start_ref, grad_middle_ref, gain_ref, lead_ref, feed_ref, up_vector_ref, result_ref, *refs,
+    block, members, pairs, grps, plans, steps, vector_stages,
+    grad_ref, qkv_ref, key_aux_ref, query_ref, out_full_ref, weight_ref, start_ref, grad_middle_ref, gain_ref, lead_ref, feed_ref, up_vector_ref, result_ref, *refs,
 ):
     count = len(plans)
     arrays = max(plan["array"] for plan in plans) + 1
     refs = list(refs)
+    firsts = members // 2
 
     def grab(n):
         found = refs[:n]
         del refs[:n]
         return found
 
-    away_refs, stay_refs = grab(arrays), grab(arrays)
-    up_ref, down_ref, output_ref, heads_ref, vectors_ref = grab(5)
+    first_refs, away_refs, stay_refs = grab(firsts), grab(arrays), grab(arrays)
+    up_ref, down_ref, output_ref, heads_ref, late_ref, early_ref = grab(6)
     own_tokens_ref, other_tokens_ref, other_result_ref, first_other = grab(4)
     grad_in, grad_s, query_s, plain_s, query_sum, out_s, joined_in = grab(7)
-    normed_s, heads_s, heads_in, heads_got, heads_sum = grab(5)
-    weight_s, joined_s, tokens_s, vectors_s = grab(4)
+    normed_s, heads_s, heads_in, heads_near, heads_got, heads_sum, heads_rows = grab(7)
+    weight_s, joined_s, tokens_s, late_s, early_s, grad_first = grab(6)
     core_in, stay_s = grab(count), grab(count)
     buffers = [grab(len(plan["stages"])) for plan in plans]
-    vector_buffers = grab(len(vector_stages))
+    late_buffers, early_buffers = grab(len(vector_stages)), grab(len(vector_stages))
     grp_count = bits(grps)
-    heads_buffers = grab(grp_count)
+    heads_buffers = grab(grp_count - 1)
     (
         local_sem, grad_send, grad_recv, out_send, out_recv, query_send, query_recv, first_send, first_recv,
-        normed_sem, weight_sem, swap_send, swap_recv, vector_send, vector_recv, far_send, far_recv,
+        normed_sem, weight_sem, swap_send, swap_recv, late_send, late_recv, early_send, early_recv, far_send, far_recv,
         heads_send, heads_recv, heads_two_send, heads_two_recv, gather_send, gather_recv, own_sem,
-    ) = grab(24)
+        near_send, near_recv, rows_send, rows_recv,
+    ) = grab(30)
     flow_sems = grab(5)
 
     rows = key_aux_ref.shape[0]
@@ -660,10 +802,15 @@
         Flow(k, plan, away_refs[plan["array"]], stay_refs[plan["array"]], core_in[k], stay_s[k], buffers[k], flow_sems)
         for k, plan in enumerate(plans)
     ]
-    vectors = FullFlow(vectors_s, vector_stages, vector_buffers, vector_send, vector_recv)
+    late = FullFlow(late_s, vector_stages, late_buffers, late_send, late_recv)
+    early = FullFlow(early_s, vector_stages, early_buffers, early_send, early_recv)
     heads_flow = FullFlow(
-        heads_sum, [("grp", b) for b in range(grp_count)], heads_buffers, heads_two_send, heads_two_recv
+        heads_near, [("grp", b) for b in range(1, grp_count)], heads_buffers, heads_two_send, heads_two_recv
     )
+    near_mine, near = flip("grp", 0)
+    near_rows = heads_near.shape[2]
+    own_rows = pl.ds(pl.multiple_of(near_mine * near_rows, near_rows), near_rows)
+    sent_rows = pl.ds(pl.multiple_of((1 - near_mine) * near_rows, near_rows), near_rows)
 
     barrier = pltpu.get_barrier_semaphore()
     greeted = [(base + other, grp) for other in others] + [(band, g) for g in groups_off] + [far]
@@ -688,9 +835,13 @@
     own.start()
     for flow in flows:
         flow.start()
-    first_copy = remote(first_ref, first_other, first_send, first_recv, core_other)
-    first_copy.start()
+    first_copies = [
+        remote(first_refs[k], first_other.at[k], first_send.at[k], first_recv.at[k], core_other) for k in range(firsts)
+    ]
+    for copy in first_copies:
+        copy.start()
     result_copy = remote(result_ref.at[1 - half], other_result_ref, swap_send.at[0], swap_recv.at[0], far)
+    result_copy.start()
 
     def weight_load(t):
         return pltpu.make_async_copy(
@@ -699,6 +850,10 @@
 
     for t in range(2):
         weight_load(t).start()
+    early_s[0:4] = feed_ref[0:4]
+    for i in range(4):
+        early_s[4 + i : 5 + i] = up_vector_ref[:, i * width : (i + 1) * width]
+    early.send()
     query_s[...] = qkv_ref[:, 0].reshape(rows, LANES)
     query_sum[...] = jnp.zeros_like(query_sum)
 
@@ -721,11 +876,28 @@
             for i, g in enumerate(groups_off)
         ]
 
+    slots = [[]]
+    for step in steps:
+        if step[0] in ("grads", "iteration", "queries"):
+            slots.append([])
+        else:
+            slots[-1].append(step)
+    rest = slots.pop()
+
+    def small_step(name, argument):
+        if name == "send":
+            flows[argument].send()
+        elif name == "early":
+            early.step()
+        elif name == "late":
+            late.step()
+        elif flows[argument].take():
+            for copy in gather_copies(argument):
+                copy.start()
+
     def advance(slot):
-        for k in slots[slot]:
-            if flows[k].advance():
-                for copy in gather_copies(k):
-                    copy.start()
+        for step in slots[slot]:
+            small_step(*step)
 
     advance(0)
     own.wait()
@@ -799,8 +971,7 @@
         def _():
             out_copy(other).start()
 
-    slot = members + 1
-    advance(slot)
+    advance(members + 1)
     out_s[:, 0] = (query_sum[...].T * scale).astype(BF16).reshape(members, block, LANES)
     for other in others:
 
@@ -810,68 +981,18 @@
 
     joined_in[me // copies] = out_s[me]
 
-    advance(slot + 1)
-    first_copy.wait()
-
     def normed_load(i):
-        source = (first_ref if i % 2 == 0 else first_other).at[i // 2]
+        source = first_refs[i // 2] if i % 2 == 0 else first_other.at[i // 2]
         return pltpu.make_async_copy(source, normed_s.at[i % 2], normed_sem.at[i % 2])
 
-    normed_load(0).start()
-    for i in range(members):
-        if i + 1 < members:
-            normed_load(i + 1).start()
-        rows_of = out_s[me ^ i]
-        rows_of = jnp.concatenate([rows_of[t] for t in range(3)], -1)
-        normed_load(i).wait()
-        term = dot_tn(rows_of, normed_s[i % 2])
-        heads_s[...] = term if i == 0 else heads_s[...] + term
-    whole = heads_s[...].T.astype(BF16).reshape(heads_in.shape)
-    heads_in[...] = jnp.where(lax.rem(me, copies) == 0, whole, jnp.zeros_like(whole))
-    heads_far = remote(heads_in.at[1 - half], heads_got, far_send, far_recv, far)
-    heads_far.start()
-    result_copy.start()
-
-    advance(slot + 2)
-    for i in range(1, pairs):
-        place = lax.rem(me // copies + i, pairs)
-        pltpu.make_async_copy(
-            joined_in.at[place, pl.ds(1, 2)], joined_in.at[place, pl.ds(1, 2)], out_recv.at[place]
-        ).wait()
-        pltpu.make_async_copy(joined_in.at[place, 0], joined_in.at[place, 0], query_recv.at[place]).wait()
-    grad_first = None
-    for t in range(3):
-        for pair in range(pairs):
-            joined_s[:, pair * LANES : (pair + 1) * LANES] = joined_in[pair, t]
-        joined = joined_s[...]
-        weight_load(t).wait()
-        term = dot_nt(joined, weight_s[t % 2])
-        grad_first = term if grad_first is None else grad_first + term
-        if t == 0:
-            weight_load(2).start()
-        if t != 1:
-            row = 4 + t // 2
-            vectors_s[row : row + 1] = jnp.sum(joined.astype(F32), 0, keepdims=True)
-    advance(slot + 3)
-    unit, inverse = normalised(start_ref[...])
-    at_input, grad_gain, grad_shift = norm_backward(grad_first, gain_ref[...], unit, inverse)
-    grad_start = at_input + grad_middle_ref[...]
-    run = tokens_s.shape[1]
-    split = grad_start.reshape(2, run, width)
-    tokens_s[...] = split.astype(BF16)
-    tokens_copy = remote(tokens_s.at[1 - half], other_tokens_ref, swap_send.at[1], swap_recv.at[1], far)
-    tokens_copy.start()
-    own_tokens_ref[...] = jnp.where(half == 0, split[0], split[1])
-    vectors_s[0:1] = jnp.sum(lead_ref[...] * grad_start, 0, keepdims=True)
-    vectors_s[1:2] = jnp.sum(grad_start, 0, keepdims=True)
-    vectors_s[2:3] = grad_gain
-    vectors_s[3:4] = grad_shift
-    vectors_s[6:10] = feed_ref[0:4]
-    for i in range(up_vector_ref.shape[1] // width):
-        vectors_s[10 + i : 11 + i] = up_vector_ref[:, i * width : (i + 1) * width]
-    for i in range(10 + up_vector_ref.shape[1] // width, vectors_s.shape[0]):
-        vectors_s[i : i + 1] = jnp.zeros((1, width), F32)
-    vectors.send()
+    def near_copy():
+        return remote(heads_in.at[:, :, sent_rows], heads_near, near_send, near_recv, near)
+
+    def far_copy():
+        return remote(heads_flow.held.at[1 - half], heads_got, far_send, far_recv, far)
+
+    def tokens_copy():
+        return remote(tokens_s.at[1 - half], other_tokens_ref, swap_send.at[1], swap_recv.at[1], far)
 
     def heads_copy(i, other):
         return remote(
@@ -879,9 +1000,72 @@
             (base + other, grp),
         )
 
-    def heads_begin():
-        heads_far.wait_recv()
-        heads_got[...] = heads_got[...] + heads_in[half]
+    def rows_copy():
+        return remote(heads_sum, heads_rows.at[:, own_rows], rows_send, rows_recv, near)
+
+    def products_step():
+        for copy in first_copies:
+            copy.wait_recv()
+        normed_load(0).start()
+        for i in range(members):
+            if i + 1 < members:
+                normed_load(i + 1).start()
+            rows_of = out_s[me ^ i]
+            rows_of = jnp.concatenate([rows_of[t] for t in range(3)], -1)
+            normed_load(i).wait()
+            term = dot_tn(rows_of, normed_s[i % 2])
+            heads_s[...] = term if i == 0 else heads_s[...] + term
+        whole = heads_s[...].T.astype(BF16).reshape(heads_in.shape)
+        heads_in[...] = jnp.where(lax.rem(me, copies) == 0, whole, jnp.zeros_like(whole))
+        near_copy().start()
+
+    def joined_step():
+        for i in range(1, pairs):
+            place = lax.rem(me // copies + i, pairs)
+            pltpu.make_async_copy(
+                joined_in.at[place, pl.ds(1, 2)], joined_in.at[place, pl.ds(1, 2)], out_recv.at[place]
+            ).wait()
+            pltpu.make_async_copy(joined_in.at[place, 0], joined_in.at[place, 0], query_recv.at[place]).wait()
+        for t in range(3):
+            for pair in range(pairs):
+                joined_s[:, pair * LANES : (pair + 1) * LANES] = joined_in[pair, t]
+            joined = joined_s[...]
+            weight_load(t).wait()
+            term = dot_nt(joined, weight_s[t % 2])
+            grad_first[...] = term if t == 0 else grad_first[...] + term
+            if t == 0:
+                weight_load(2).start()
+            if t != 1:
+                row = 4 + t // 2
+                late_s[row : row + 1] = jnp.sum(joined.astype(F32), 0, keepdims=True)
+
+    def start_step():
+        unit, inverse = normalised(start_ref[...])
+        at_input, grad_gain, grad_shift = norm_backward(grad_first[...], gain_ref[...], unit, inverse)
+        grad_start = at_input + grad_middle_ref[...]
+        split = grad_start.reshape((2,) + own_tokens_ref.shape)
+        tokens_s[...] = split.astype(BF16)
+        tokens_copy().start()
+        own_tokens_ref[...] = jnp.where(half == 0, split[0], split[1])
+        lead = jnp.concatenate([lead_ref[...]] * (width // LANES), -1)
+        late_s[0:1] = jnp.sum(lead * grad_start, 0, keepdims=True)
+        late_s[1:2] = jnp.sum(grad_start, 0, keepdims=True)
+        late_s[2:3] = grad_gain
+        late_s[3:4] = grad_shift
+        late_s[6:8] = jnp.zeros((2, width), F32)
+        late.send()
+
+    def near_step():
+        near_copy().wait_recv()
+        heads_near[...] = heads_near[...] + heads_in[:, :, own_rows]
+        heads_flow.send()
+        while heads_flow.at < len(heads_flow.stages):
+            heads_flow.step()
+        far_copy().start()
+
+    def far_step():
+        far_copy().wait_recv()
+        heads_got[...] = heads_got[...] + heads_flow.held[half]
 
         @pl.when(lax.rem(me, copies) == 0)
         def _():
@@ -889,33 +1073,34 @@
                 heads_copy(i, other).start()
             heads_sum[me // copies] = heads_got[me]
 
-    def heads_middle():
+    def members_step():
         for place in range(pairs):
 
             @pl.when(place * copies != me)
             def _():
                 pltpu.make_async_copy(heads_sum.at[place], heads_sum.at[place], heads_recv.at[place]).wait()
 
-        heads_flow.send()
-
-    def heads_end():
-        while heads_flow.at < len(heads_flow.stages):
-            heads_flow.step()
+        rows_copy().start()
+        heads_rows[:, own_rows] = heads_sum[...]
+
+    def rows_step():
+        rows_copy().wait_recv()
         for pair in range(pairs):
             for t in range(3):
                 column = t * width + pair * LANES
-                heads_ref[:, column : column + LANES] = heads_flow.held[pair, :, t * LANES : (t + 1) * LANES]
-
-    extra = [heads_begin, vectors.step, heads_middle, vectors.step, heads_end] + [vectors.step] * len(vector_stages)
-    for n, k in enumerate(slots[slot + 4]):
-        if flows[k].advance():
-            for copy in gather_copies(k):
-                copy.start()
-        if n % 2 == 1 and extra:
-            extra.pop(0)()
-    while extra:
-        extra.pop(0)()
-    vectors_ref[...] = vectors.held[...]
+                heads_ref[:, column : column + LANES] = heads_rows[pair, :, t * LANES : (t + 1) * LANES]
+
+    large = {
+        "products": products_step, "joined": joined_step, "start": start_step, "near": near_step,
+        "far": far_step, "members": members_step, "rows": rows_step,
+    }
+    for name, argument in rest:
+        if name in large:
+            large[name]()
+        else:
+            small_step(name, argument)
+    late_ref[...] = late.held[...]
+    early_ref[...] = early.held[...]
 
     for copy in grad_copies:
         copy.wait_send()
@@ -931,11 +1116,15 @@
         for i, other in enumerate(others):
             heads_copy(i, other).wait_send()
 
-    for flow in flows + [vectors, heads_flow]:
+    for flow in flows + [late, early, heads_flow]:
         flow.drain()
-    heads_far.wait_send()
+    near_copy().wait_send()
+    rows_copy().wait_send()
+    far_copy().wait_send()
+    for copy in first_copies:
+        copy.wait_send()
     result_copy.wait()
-    tokens_copy.wait()
+    tokens_copy().wait()
     for k in range(count):
         for copy in gather_copies(k):
             copy.wait()
@@ -952,36 +1141,35 @@
     held = width // bands
     inner = up_vector.shape[1]
     arrays, count, grp_count = len(away), len(plans), bits(grps)
-    shapes = [Flow.shapes(plan) for plan in plans]
     z_low = bits(bands) - 2
     links = {("band", z_low): "z", ("band", z_low + 1): "Z"}
-    link = lambda stage: links.get(stage, "y" if stage[0] == "grp" else "x")
-    size = lambda shape: 2 * functools.reduce(lambda m, n: m * n, shape, 1) / 2**20
-    longer = rows / 2048
-    tasks = [8.0] + [3.4 * longer] * members + [2.0, 4.0 * longer, 5.0, 4.0]
-    slots = plan_events(
-        [(size(found[0]), [link(stage) for stage in plan["stages"]]) for found, plan in zip(shapes, plans)], tasks
-    )
+    links.update({("band", b): "x" for b in range(1, z_low)})
+    links.update({("grp", b): "y" for b in range(grp_count)})
     vector_stages = [("band", b) for b in range(bits(bands))] + [("grp", b) for b in range(grp_count)]
+    sizes = [2**bits(bands) * plan["rows"][1] * plan["columns"][1] / 2**20 for plan in plans]
+    orders, steps, _, _ = plan_steps(sizes, links, vector_stages, members, 4.0 * rows / 2048, 7.0, 5.0)
+    plans = [dict(plan, stages=order) for plan, order in zip(plans, orders)]
+    shapes = [Flow.shapes(plan) for plan in plans]
     longest = max(len(plan["stages"]) for plan in plans)
     vmem = pl.BlockSpec(memory_space=pltpu.VMEM)
     anywhere = pl.BlockSpec(memory_space=pl.ANY)
     dma = pltpu.SemaphoreType.DMA
     return pl.pallas_call(
-        functools.partial(backward_kernel, block, members, pairs, grps, plans, slots, vector_stages),
+        functools.partial(backward_kernel, block, members, pairs, grps, plans, steps, vector_stages),
         out_shape=(
             jax.ShapeDtypeStruct((held, inner), BF16),
             jax.ShapeDtypeStruct((inner // bands, width), BF16),
             jax.ShapeDtypeStruct((held, width), BF16),
             jax.ShapeDtypeStruct((held, 3 * width), BF16),
-            jax.ShapeDtypeStruct((16, width), F32),
+            jax.ShapeDtypeStruct((8, width), F32),
+            jax.ShapeDtypeStruct((8, width), F32),
             jax.ShapeDtypeStruct((run, width), F32),
             jax.ShapeDtypeStruct((run, width), BF16),
             jax.ShapeDtypeStruct((run, width), BF16),
-            jax.ShapeDtypeStruct(first.shape, BF16),
+            jax.ShapeDtypeStruct((len(first),) + first[0].shape, BF16),
         ),
-        in_specs=[anywhere] + [vmem] * 4 + [anywhere] * 2 + [vmem] * 6 + [anywhere] * (1 + 2 * arrays),
-        out_specs=(anywhere, anywhere, anywhere, vmem, vmem, vmem, anywhere, anywhere, anywhere),
+        in_specs=[anywhere] + [vmem] * 4 + [anywhere] + [vmem] * 6 + [anywhere] * (1 + len(first) + 2 * arrays),
+        out_specs=(anywhere, anywhere, anywhere, vmem, vmem, vmem, vmem, anywhere, anywhere, anywhere),
         scratch_shapes=[
             pltpu.VMEM((members, 1, block, LANES), BF16),
             pltpu.VMEM((2, rows, LANES), BF16),
@@ -993,36 +1181,117 @@
             pltpu.VMEM((2, block, width), BF16),
             pltpu.VMEM((3 * LANES, width), F32),
             pltpu.VMEM((2, members, held, 3 * LANES), BF16),
-            pltpu.VMEM((members, held, 3 * LANES), BF16),
+            pltpu.VMEM((2, members, held // 2, 3 * LANES), BF16),
+            pltpu.VMEM((members, held // 2, 3 * LANES), BF16),
+            pltpu.VMEM((pairs, held // 2, 3 * LANES), BF16),
             pltpu.VMEM((pairs, held, 3 * LANES), BF16),
             pltpu.VMEM((2, width, width), BF16),
             pltpu.VMEM((total, width), BF16),
             pltpu.VMEM((2, run, width), BF16),
-            pltpu.VMEM((16, width), F32),
+            pltpu.VMEM((8, width), F32),
+            pltpu.VMEM((8, width), F32),
+            pltpu.VMEM((total, width), F32),
         ]
         + [pltpu.VMEM(found[0], BF16) for found in shapes]
         + [pltpu.VMEM(found[1], BF16) for found in shapes]
         + [pltpu.VMEM(shape, BF16) for found in shapes for shape in found[1:]]
-        + [pltpu.VMEM((16, width), F32) for _ in vector_stages]
-        + [pltpu.VMEM((pairs, held, 3 * LANES), BF16) for _ in range(grp_count)]
+        + [pltpu.VMEM((8, width), F32) for _ in vector_stages * 2]
+        + [pltpu.VMEM((2, members, held // 2, 3 * LANES), BF16) for _ in range(grp_count - 1)]
         + [
             dma, dma((members,)), dma((members,)), dma((members,)), dma((members,)), dma((members,)), dma((members,)),
-            dma, dma, dma((2,)), dma((2,)), dma((2,)), dma((2,)),
-            dma((len(vector_stages),)), dma((len(vector_stages),)), dma, dma,
+            dma((len(first),)), dma((len(first),)), dma((2,)), dma((2,)), dma((2,)), dma((2,)),
+            dma((len(vector_stages),)), dma((len(vector_stages),)), dma((len(vector_stages),)),
+            dma((len(vector_stages),)), dma, dma,
             dma((members,)), dma((pairs,)), dma((grp_count,)), dma((grp_count,)),
-            dma((count, grps)), dma((count, grps)), dma((count,)),
+            dma((count, grps)), dma((count, grps)), dma((count,)), dma, dma, dma, dma,
         ]
         + [dma((count,)), dma((count,)), dma((count,)), dma((count, longest)), dma((count, longest))],
         compiler_params=pltpu.CompilerParams(
-            vmem_limit_bytes=60 * 2**20, collective_id=collective_id, has_side_effects=True
+            vmem_limit_bytes=62 * 2**20, collective_id=collective_id, has_side_effects=True
         ),
         cost_estimate=pl.CostEstimate(
             flops=24 * rows * rows * LANES, bytes_accessed=64 * 2**20, transcendentals=2 * rows * rows
         ),
         name="backward",
     )(
-        grad_blocks, qkv, key_aux, query, out_full, first, weight, start, grad_middle, gain.reshape(1, width),
-        lead_rows, feed_vectors, up_vector, result.reshape(2, run, width), *away, *stay,
+        grad_blocks, qkv, key_aux, query, out_full, weight, start, grad_middle, gain.reshape(1, width),
+        lead_rows, feed_vectors, up_vector, result.reshape(2, run, width), *first, *away, *stay,
+    )
+
+
+SMALL_ROWS = (0, 1, 2, 3, 4, 5, 8, 9, 10, 11)
+
+
+def emit_kernel(
+    bands, up_ref, down_ref, output_ref, heads_ref, own_grads_ref, other_grads_ref, result_ref,
+    other_result_ref, late_ref, early_ref,
+    up_out, down_out, output_out, heads_out, grads_out, result_out, up_vector_out, *small_outs,
+):
+    band = lax.axis_index("band")
+    held = late_ref.shape[1] // bands
+    half = band // (bands // 2)
+    up_out[...] = up_ref[...].astype(F32)
+    down_out[...] = down_ref[...].astype(F32)
+    output_out[...] = output_ref[...].astype(F32)
+    heads_out[...] = heads_ref[...].astype(F32)
+    own, other = own_grads_ref[...], other_grads_ref[...].astype(F32)
+    grads_out[0] = jnp.where(half == 0, own, other)
+    grads_out[1] = jnp.where(half == 0, other, own)
+    other = other_result_ref[...]
+    result_out[0] = jnp.where(half == 0, result_ref[0], other)
+    result_out[1] = jnp.where(half == 0, other, result_ref[1])
+
+    @pl.when(pl.program_id(0) == 0)
+    def _():
+        size = late_ref.shape[1] // bands
+        here = pl.ds(pl.multiple_of(band * held // LANES * LANES, LANES), LANES)
+        both = jnp.concatenate([late_ref[:, here], early_ref[:, here]], 0)
+        value = both[:, :size]
+        for i in range(1, LANES // size):
+            value = jnp.where(lax.rem(band, LANES // size) == i, both[:, i * size : (i + 1) * size], value)
+        for i, out in enumerate(small_outs):
+            out[...] = value[SMALL_ROWS[i] : SMALL_ROWS[i] + 1]
+        columns = up_vector_out.shape[1]
+        spread = late_ref.shape[1] // columns
+        at = pl.ds(pl.multiple_of(lax.rem(band, spread) * columns, columns), columns)
+        value = early_ref[4:5, at]
+        for i in range(1, 4):
+            value = jnp.where(band // spread == i, early_ref[4 + i : 5 + i, at], value)
+        up_vector_out[...] = value
+
+
+def emit(up, down, output, heads, own_grads, other_grads, result, other_result, late, early, bands):
+    run, width = own_grads.shape
+    size = width // bands
+    columns = 4 * width // bands
+    steps = 2
+    by_rows = lambda shape: pl.BlockSpec(
+        shape[:-2] + (shape[-2] // steps, shape[-1]), lambda i: (0,) * (len(shape) - 2) + (i, 0)
+    )
+    matrices = (up, down, output, heads)
+    both = (2, run, width)
+    return pl.pallas_call(
+        functools.partial(emit_kernel, bands),
+        grid=(steps,),
+            in_specs=[by_rows(m.shape) for m in matrices]
+            + [by_rows((run, width)), by_rows((run, width)), by_rows(both), by_rows((run, width))]
+            + [constant(8, width)] * 2,
+            out_specs=tuple(by_rows(m.shape) for m in matrices)
+            + (by_rows(both), by_rows(both), constant(1, columns))
+            + (constant(1, size),) * len(SMALL_ROWS),
+        out_shape=tuple(jax.ShapeDtypeStruct(m.shape, F32) for m in matrices)
+        + (
+            jax.ShapeDtypeStruct(both, F32),
+            jax.ShapeDtypeStruct(both, BF16),
+            jax.ShapeDtypeStruct((1, columns), F32),
+        )
+        + (jax.ShapeDtypeStruct((1, size), F32),) * len(SMALL_ROWS),
+        compiler_params=pltpu.CompilerParams(vmem_limit_bytes=VMEM_BYTES),
+        cost_estimate=pl.CostEstimate(flops=0, bytes_accessed=8 * 2**20, transcendentals=0),
+        name="emit",
+    )(
+        up, down, output, heads, own_grads, other_grads,
+        result.reshape(both), other_result, late, early,
     )
 
 
@@ -1081,44 +1350,18 @@
     own_group = bit_of(far)
     block = total
 
-    def regroup(array):
-        mine, theirs = take(array, 0, own_group), swap(take(array, 0, 1 - own_group), far)
-        low = jnp.where(own_group == 0, mine, theirs)
-        high = jnp.where(own_group == 0, theirs, mine)
-        return jnp.concatenate([low, high], 0)
-
-    def by_member(array):
-        return take(array, 0, own_group).reshape(groups, members, rows).transpose(1, 0, 2)
-
-    own_tokens = regroup(tokens)
-    seg_rows, valid_rows = by_member(segment), by_member(valid)
-    local_seg = take(seg_rows, 0, lax.rem(band, members)).reshape(total, 1)
-    lead_days = take(lead_index, 0, own_group).astype(F32) * 0.25
-    lead_rows = jnp.where(local_seg == 0, lead_days[0], lead_days[1])
-    seg_own, valid_own = seg_rows.reshape(-1), valid_rows.reshape(-1)
-    spare = jnp.arange(LANES, dtype=jnp.int32)[None, :] % HEAD_DIM
-    query_aux = (spare == seg_own[:, None]).astype(BF16)
-    allowed = (spare == seg_own[:, None]) & (valid_own[:, None] == 1)
-    key_aux = jnp.where(
-        spare < 2, jnp.where(allowed, 0.0, MASKED), jnp.where(spare < 5, 1.0, 0.0)
-    ).astype(BF16)
     core = lax.rem(band, 2).astype(jnp.int32).reshape(1)
-    head_bias = jnp.stack([query_bias, jnp.zeros_like(query_bias), value_bias]).reshape(3, 1, width)
-
-    late_tokens = after(own_tokens, query_aux, key_aux, head_bias, lead_rows)
-    grad_out = regroup(after(cotangent, own_tokens))
-    start, first_low, blocks = heads_forward(
-        late_tokens, lead_rows, lead_weight, lead_bias, first_gain, first_shift, heads_weight, head_bias
+    qkv, attended, grad_out, start, first_low, lead_rows, key_aux, out_full, query_marked = forward(
+        tokens, cotangent, lead_index, segment, valid, lead_weight, lead_bias, first_gain, first_shift,
+        heads_weight, query_bias, value_bias, members, 1,
     )
-    qkv, attended, out_full, query_marked = attention_forward(blocks, query_aux, key_aux, members, 1)
-    attended = after(attended, grad_out)
 
     def normed_of(offset):
         return lax.ppermute(
             after(first_low, attended), "band", [(i, i ^ offset) for i in range(bands)]
         )
 
-    first_rows = jnp.stack([first_low] + [normed_of(2 * k) for k in range(1, members // 2)])
+    first_rows = [first_low] + [normed_of(2 * k) for k in range(1, members // 2)]
 
     (
         result, grad_middle, grad_blocks, down_away, down_stay, up_away, up_stay,
@@ -1130,65 +1373,39 @@
     split = lambda v: v.reshape((2,) * (bits(bands) - 1) + v.shape[1:])
     held_up, held_down, inner = up_stay.shape[1], down_stay.shape[1], up_weight.shape[1]
     lead = [b for b in range(1, bits(bands))][::-1]
-    along = {
-        "x": [("band", b) for b in range(1, bits(bands) - 2)],
-        "y": [("grp", b) for b in range(bits(grps))],
-        "z": [("band", bits(bands) - 2)],
-        "Z": [("band", bits(bands) - 1)],
-    }
-
-    def plan(array, rows_of, columns_of, links):
-        stages = [stage for link in links for stage in along[link]]
-        return {"array": array, "rows": rows_of, "columns": columns_of, "lead": lead, "stages": stages}
+
+    def plan(array, rows_of, columns_of):
+        return {"array": array, "rows": rows_of, "columns": columns_of, "lead": lead}
 
     quarter, fourth = inner // 4, held_down // 4
-    up_part = lambda i, links: plan(0, (0, held_up), (i * quarter, quarter), links)
-    down_part = lambda i, links: plan(1, (i * fourth, fourth), (0, width), links)
-    plans = [
-        up_part(0, "yzZx"),
-        up_part(1, "xyzZ"),
-        up_part(2, "zxyZ"),
-        up_part(3, "xyzZ"),
-        down_part(0, "xyzZ"),
-        down_part(1, "yzZx"),
-        down_part(2, "zxyZ"),
-        down_part(3, "xyzZ"),
-        plan(2, (0, held_up), (0, width), "yzZx"),
-    ]
-    grad_up, grad_down, grad_output, grad_heads, vectors, own_grads, other_grads, other_result, _ = backward(
+    plans = []
+    for i in range(4):
+        plans.append(plan(0, (0, held_up), (i * quarter, quarter)))
+        plans.append(plan(1, (i * fourth, fourth), (0, width)))
+    plans.append(plan(2, (0, held_up), (0, width)))
+    grad_up, grad_down, grad_output, grad_heads, late, early, own_grads, other_grads, other_result, _ = backward(
         grad_blocks, qkv, key_aux, query_marked, out_full, first_rows, heads_weight, start, grad_middle,
         first_gain, lead_rows, feed_vectors, grad_up_bias, result,
         [split(v) for v in (up_away, down_away, output_away)],
         [split(v) for v in (up_stay, down_stay, output_stay)],
         plans, pairs, bands, grps, 3,
     )
-    own_result = take(result.reshape(2, rows, width), 0, own_group)
-
-    def assemble(mine, theirs):
-        theirs = theirs.astype(mine.dtype)
-        low, high = jnp.where(own_group == 0, mine, theirs), jnp.where(own_group == 0, theirs, mine)
-        return jnp.stack([low, high])
-
-    small = take(vectors[:10].reshape(10, bands, width // bands), 1, band)
-    grad_up_bias = take(vectors[10 : 10 + up_weight.shape[1] // width].reshape(bands, -1), 0, band)
-    wide = lambda v: v.astype(F32)
+    grad_up, grad_down, grad_output, grad_heads, grad_tokens, outcome, *vectors = emit(
+        grad_up, grad_down, grad_output, grad_heads, own_grads, other_grads, result, other_result,
+        late, early, bands,
+    )
+    grad_up_bias, *small = [v.reshape(-1) for v in vectors]
     return (
-        assemble(own_result, other_result),
-        assemble(own_grads, other_grads),
-        small[0],
-        small[1],
-        small[2],
-        small[3],
-        wide(grad_heads),
-        small[4],
-        small[5],
-        wide(grad_output),
-        small[6],
-        small[7],
-        small[8],
-        wide(grad_up),
+        outcome,
+        grad_tokens,
+        *small[:4],
+        grad_heads,
+        *small[4:6],
+        grad_output,
+        *small[6:9],
+        grad_up,
         grad_up_bias,
-        wide(grad_down),
+        grad_down,
         small[9],
     )
 

time: 251 us -> 209 us (0.83); the launches traced: 247 us -> 209 us
  other arithmetic: 18.3 us -> 0 us
  Pallas kernels: 213 us -> 203 us
  starting transfers between devices: 7.66 us -> 3.55 us
  local copies, waits for them, and re-layouts: 4.68 us -> 1.09 us
  waiting for transfers between devices: 2.83 us -> 0.01 us
    pallas_call x1, Pallas kernels: 139 us -> 123 us  [backward(): pl.pallas_call(functools.partial(backward_kernel, block, members, pairs,...]
    pallas_call x2, Pallas kernels: 47.4 us -> 55.9 us  [the longest x1 51.9 us: forward(): pl.pallas_call(functools.partial(forward_kernel, block, members, pairs),...]
    convert_element_type x6 -> x0, other arithmetic: 8.31 us -> none  [the longest x4 4.9 us: local(): wide = lambda v: v.astype(F32)]
    another operation x6 -> x0, other arithmetic: 5.48 us -> none  [the longest x4 3.11 us: assemble(): return jnp.stack([low, high])]
    ppermute x2 -> x0, starting transfers between devices: 4.17 us -> none  [swap(): return lax.ppermute(array, axis, [(i, i ^ 1 << bit) for i in range(size)])]
    ppermute x2 -> x0, waiting for transfers between devices: 2.82 us -> none  [swap(): return lax.ppermute(array, axis, [(i, i ^ 1 << bit) for i in range(size)])]
  transfers between devices with their start and end apart: 5 -> 3, of which waited for: 1 -> 0; matrix products, arithmetic and copies ran while one was open for 4% -> 0% of each run, Pallas kernels for 30% -> 12%
where the time goes in v2:
time: 209 us
  Pallas kernels  203 us (97%)
  starting transfers between devices  3.55 us (2%)
    pallas_call x1, Pallas kernels, backward(): pl.pallas_call(functools.partial(backward_kernel, block, members, pairs,...  123 us
    pallas_call x1, Pallas kernels, forward(): pl.pallas_call(functools.partial(forward_kernel, block, members, pairs),...  51.9 us
    pallas_call x1, Pallas kernels, feed(): pl.pallas_call(feed_kernel, grid_spec=pltpu.PrefetchScalarGridSpec(num_sc...  24.6 us
  transfers between devices with their start and end apart: 3, of which 0 were waited for; matrix products, arithmetic and copies ran while one was open for 0% of the time, Pallas kernels for 12%

profile of v2, /device:TPU:0, one launch (start us, length us, event | category | flops | bytes accessed | tf_op | source)
XLA Modules:
  0.0 208.9 jit_solution(6118493096739802562)
XLA Ops:
  0.7 51.9 %forward.1 = (bf16[8,3,256,128]{3,2,1,0:T(8,128)(2,1)}, bf16[8,1,256,128]{3,2,1,0:T(8,128)(2,1)}, bf16[256,1024]{1,0:T(8,128)(2,1)}, f32[256,1024]{1,0:T(8,128)}...) custom-call(bf16[2,128,1024]{2,1,0:T(8,128)(2,1)} %tokens_ref.1, ...), custom_call_target="tpu_custom_call" | custom-call | flops 4294967296 | bytes 33554432 | tf_op jit(solution)/shard_map/forward/pallas_call | solution.py:273
  52.6 0.1 collective-permute-start.2
  52.7 2.1 collective-permute-start.1
  54.7 1.4 collective-permute-start
  56.2 24.6 %feed.1 = (bf16[256,1024]{1,0:T(8,128)(2,1)}, f32[256,1024]{1,0:T(8,128)}, bf16[8,1,256,128]{3,2,1,0:T(8,128)(2,1)}, bf16[8,256,1024]{2,1,0:T(8,128)(2,1)}, bf16...) custom-call(s32[1]{0:T(128)} %bitcast.core_ref, ...), custom_call_target="tpu_custom_call" | custom-call | flops 12884901888 | bytes 33554432 | tf_op jit(solution)/shard_map/feed/pallas_call | solution.py:424
  80.8 0.0 collective-permute-done.2.refs_3_
  80.8 0.0 copy-start
  80.8 0.0 collective-permute-done.1.refs_2_
  80.8 0.0 copy-start.1
  80.8 0.0 collective-permute-done.refs_1_
  80.8 0.0 copy-start.2
  80.8 0.8 copy-done
  81.6 0.2 copy-done.1
  81.8 0.2 copy-done.2
  81.9 122.8 %backward.1 = (bf16[64,4096]{1,0:T(8,128)(2,1)}, bf16[256,1024]{1,0:T(8,128)(2,1)}, bf16[64,1024]{1,0:T(8,128)(2,1)}, bf16[64,3072]{1,0:T(8,128)(2,1)}, f32[8,10...) custom-call(bf16[8,1,256,128]{3,2,1,0:T(8,128)(2,1)} %get-tuple-elem, ...), custom_call_target="tpu_custom_call" | custom-call | flops 12884901888 | bytes 67108864 | tf_op jit(solution)/shard_map/backward/pallas_call | solution.py:1157
  204.8 3.9 %emit.1 = (f32[64,4096]{1,0:T(8,128)}, f32[256,1024]{1,0:T(8,128)}, f32[64,1024]{1,0:T(8,128)}, f32[64,3072]{1,0:T(8,128)}, f32[2,128,1024]{2,1,0:T(8,128)}, /*i...) custom-call(bf16[64,4096]{1,0:T(8,128)(2,1)} %get-tuple-element.85.u, ...), custom_call_target="tpu_custom_call" | custom-call | bytes 8388608 | tf_op jit(solution)/shard_map/emit/pallas_call | solution.py:1273
Async XLA Ops:
  52.6 28.2 %collective-permute-start.2 = (bf16[256,1024]{1,0:T(8,128)(2,1)}, bf16[256,1024]{1,0:T(8,128)(2,1)S(1)}, u32[]{:S(2)}, u32[]{:S(2)}) collective-permute-start(bf16[256,1024]{1,0:T(8,128)(2,1)} %get-tuple-element.78.refs_0_), channel_id=1, source_target_pairs={{0,12},{2,14},{4,8},{6,10},{8,4},{10,6},{12,0},{14,2},{16,28},{18,... | collective-permute-start | bytes 1572872 | tf_op jit(solution)/shard_map/ppermute | solution.py:1360
  52.7 28.1 %collective-permute-start.1 = (bf16[256,1024]{1,0:T(8,128)(2,1)}, bf16[256,1024]{1,0:T(8,128)(2,1)S(1)}, u32[]{:S(2)}, u32[]{:S(2)}) collective-permute-start(bf16[256,1024]{1,0:T(8,128)(2,1)} %get-tuple-element.78.refs_0_), channel_id=1, source_target_pairs={{0,8},{2,10},{4,12},{6,14},{8,0},{10,2},{12,4},{14,6},{16,24},{18,... | collective-permute-start | bytes 1572872 | tf_op jit(solution)/shard_map/ppermute | solution.py:1360
  54.7 26.1 %collective-permute-start = (bf16[256,1024]{1,0:T(8,128)(2,1)}, bf16[256,1024]{1,0:T(8,128)(2,1)S(1)}, u32[]{:S(2)}, u32[]{:S(2)}) collective-permute-start(bf16[256,1024]{1,0:T(8,128)(2,1)} %get-tuple-element.78.refs_0_), channel_id=1, source_target_pairs={{0,4},{2,6},{4,0},{6,2},{8,12},{10,14},{12,8},{14,10},{16,20},{18,... | collective-permute-start | bytes 1572872 | tf_op jit(solution)/shard_map/ppermute | solution.py:1360
  80.8 0.8 copy-start
  80.8 1.0 copy-start.1
  80.8 1.1 copy-start.2

commit v3 on v2

--- a/solution.py
+++ b/solution.py
@@ -182,6 +182,8 @@
         for phase in range(2):
             qkv_copy(2, phase, i, other).wait_recv()
     value_s[...] = qkv_in[:, 2].reshape(rows, LANES)
+    keep = pltpu.make_async_copy(qkv_in.at[:, pl.ds(1, 2)], qkv_ref.at[:, pl.ds(1, 2)], keep_sem)
+    keep.start()
 
     def sends_to(other):
         return (lax.rem(other, copies) == lax.rem(me, copies)) & (other != me)
@@ -233,13 +235,14 @@
         def _():
             grads_swap.start()
 
-    keep = pltpu.make_async_copy(qkv_in, qkv_ref, keep_sem)
-    keep.start()
     own_out = pltpu.make_async_copy(out_s.at[me], attended_ref.at[me // copies], token_sem)
     own_out.start()
+    queries = pltpu.make_async_copy(qkv_in.at[:, 0], qkv_ref.at[:, 0], local_sem)
     keep.wait()
     own_out.wait()
     grads_own.wait()
+    queries.start()
+    queries.wait()
     tokens_swap.wait_send()
     for t in range(3):
         for phase in range(2):

time: 209 us -> 209 us (level)
  no operation moved by 1% of the time
where the time goes in v3:
time: 209 us
  Pallas kernels  203 us (97%)
  starting transfers between devices  3.55 us (2%)
    pallas_call x1, Pallas kernels, backward(): pl.pallas_call(functools.partial(backward_kernel, block, members, pairs,...  123 us
    pallas_call x1, Pallas kernels, forward(): pl.pallas_call(functools.partial(forward_kernel, block, members, pairs),...  51.9 us
    pallas_call x1, Pallas kernels, feed(): pl.pallas_call(feed_kernel, grid_spec=pltpu.PrefetchScalarGridSpec(num_sc...  24.6 us
  transfers between devices with their start and end apart: 3, of which 0 were waited for; matrix products, arithmetic and copies ran while one was open for 0% of the time, Pallas kernels for 12%

profile of v3, /device:TPU:0, one launch (start us, length us, event | category | flops | bytes accessed | tf_op | source)
XLA Modules:
  0.0 208.9 jit_solution(16902463403439809842)
XLA Ops:
  0.7 51.9 %forward.1 = (bf16[8,3,256,128]{3,2,1,0:T(8,128)(2,1)}, bf16[8,1,256,128]{3,2,1,0:T(8,128)(2,1)}, bf16[256,1024]{1,0:T(8,128)(2,1)}, f32[256,1024]{1,0:T(8,128)}...) custom-call(bf16[2,128,1024]{2,1,0:T(8,128)(2,1)} %tokens_ref.1, ...), custom_call_target="tpu_custom_call" | custom-call | flops 4294967296 | bytes 33554432 | tf_op jit(solution)/shard_map/forward/pallas_call | solution.py:276
  52.6 0.1 collective-permute-start.2
  52.7 2.1 collective-permute-start.1
  54.7 1.4 collective-permute-start
  56.2 24.6 %feed.1 = (bf16[256,1024]{1,0:T(8,128)(2,1)}, f32[256,1024]{1,0:T(8,128)}, bf16[8,1,256,128]{3,2,1,0:T(8,128)(2,1)}, bf16[8,256,1024]{2,1,0:T(8,128)(2,1)}, bf16...) custom-call(s32[1]{0:T(128)} %bitcast.core_ref, ...), custom_call_target="tpu_custom_call" | custom-call | flops 12884901888 | bytes 33554432 | tf_op jit(solution)/shard_map/feed/pallas_call | solution.py:427
  80.8 0.0 collective-permute-done.2.refs_3_
  80.8 0.0 copy-start
  80.8 0.0 collective-permute-done.1.refs_2_
  80.8 0.0 copy-start.1
  80.8 0.0 collective-permute-done.refs_1_
  80.8 0.0 copy-start.2
  80.8 0.8 copy-done
  81.6 0.2 copy-done.1
  81.8 0.2 copy-done.2
  81.9 122.8 %backward.1 = (bf16[64,4096]{1,0:T(8,128)(2,1)}, bf16[256,1024]{1,0:T(8,128)(2,1)}, bf16[64,1024]{1,0:T(8,128)(2,1)}, bf16[64,3072]{1,0:T(8,128)(2,1)}, f32[8,10...) custom-call(bf16[8,1,256,128]{3,2,1,0:T(8,128)(2,1)} %get-tuple-elem, ...), custom_call_target="tpu_custom_call" | custom-call | flops 12884901888 | bytes 67108864 | tf_op jit(solution)/shard_map/backward/pallas_call | solution.py:1160
  204.8 3.9 %emit.1 = (f32[64,4096]{1,0:T(8,128)}, f32[256,1024]{1,0:T(8,128)}, f32[64,1024]{1,0:T(8,128)}, f32[64,3072]{1,0:T(8,128)}, f32[2,128,1024]{2,1,0:T(8,128)}, /*i...) custom-call(bf16[64,4096]{1,0:T(8,128)(2,1)} %get-tuple-element.85.u, ...), custom_call_target="tpu_custom_call" | custom-call | bytes 8388608 | tf_op jit(solution)/shard_map/emit/pallas_call | solution.py:1276
Async XLA Ops:
  52.6 28.2 %collective-permute-start.2 = (bf16[256,1024]{1,0:T(8,128)(2,1)}, bf16[256,1024]{1,0:T(8,128)(2,1)S(1)}, u32[]{:S(2)}, u32[]{:S(2)}) collective-permute-start(bf16[256,1024]{1,0:T(8,128)(2,1)} %get-tuple-element.78.refs_0_), channel_id=1, source_target_pairs={{0,12},{2,14},{4,8},{6,10},{8,4},{10,6},{12,0},{14,2},{16,28},{18,... | collective-permute-start | bytes 1572872 | tf_op jit(solution)/shard_map/ppermute | solution.py:1363
  52.7 28.1 %collective-permute-start.1 = (bf16[256,1024]{1,0:T(8,128)(2,1)}, bf16[256,1024]{1,0:T(8,128)(2,1)S(1)}, u32[]{:S(2)}, u32[]{:S(2)}) collective-permute-start(bf16[256,1024]{1,0:T(8,128)(2,1)} %get-tuple-element.78.refs_0_), channel_id=1, source_target_pairs={{0,8},{2,10},{4,12},{6,14},{8,0},{10,2},{12,4},{14,6},{16,24},{18,... | collective-permute-start | bytes 1572872 | tf_op jit(solution)/shard_map/ppermute | solution.py:1363
  54.7 26.1 %collective-permute-start = (bf16[256,1024]{1,0:T(8,128)(2,1)}, bf16[256,1024]{1,0:T(8,128)(2,1)S(1)}, u32[]{:S(2)}, u32[]{:S(2)}) collective-permute-start(bf16[256,1024]{1,0:T(8,128)(2,1)} %get-tuple-element.78.refs_0_), channel_id=1, source_target_pairs={{0,4},{2,6},{4,0},{6,2},{8,12},{10,14},{12,8},{14,10},{16,20},{18,... | collective-permute-start | bytes 1572872 | tf_op jit(solution)/shard_map/ppermute | solution.py:1363
  80.8 0.8 copy-start
  80.8 1.0 copy-start.1
  80.8 1.1 copy-start.2
